TPU v7x, 256 devices: a whole 4x4x8 slice. The times are simulated.
256 devices in a mesh: dp: 16 (over z, core), mp: 16 (over y, x).
Axes of the slice: x: 4, y: 4, z: 8, core: 2. Of those that a mesh axis runs over, the one named last changes fastest.
Arguments:
- features: bfloat16 [6144, 2048], P('dp', 'mp'), may hold values from -6 to 6
- w_in: bfloat16 [2048, 16384], P('dp', 'mp'), may hold values from -0.125 to 0.125
- w_out: bfloat16 [16384, 2048], P('mp', 'dp'), may hold values from -0.0625 to 0.0625
- unit_order: int32 [16384], P('mp'), may hold values from 0 to 16383, as said below
- cotangents: bfloat16 [4, 6144, 2048], P(None, 'dp', 'mp'), may hold values from -6 to 6
Outputs:
- outputs: bfloat16 [4, 6144, 2048], P(None, 'dp', 'mp')
- grad_features: bfloat16 [6144, 2048], P('dp', 'mp')
- grad_in: bfloat16 [2048, 16384], P('dp', 'mp')
- grad_out: bfloat16 [16384, 2048], P('mp', 'dp')
Inputs may be any that keep to these rules, and one draw needn't show every extreme that they name: `unit_order`: A permutation of 0 to 16383; every block of 1024 consecutive stored positions holds exactly 128 units below 2048, 128 from 2048 to 4096, 256 from 4096 to 8192 and 512 from 8192 up.
All inputs are finite; a program needn't handle non-finite values.
Results may differ from a plain program's by a relative error of at most 0.023.
Values may be sent and summed in bfloat16 or wider, within the bound.
No kernel may reach another device: no remote copies, remote signals or barrier semaphores. Data moves between devices by JAX's collectives and lax.ppermute only.
A program may use at most 128 MiB of HBM per device.

v0:
```python
import jax
import jax.numpy as jnp
from jax import lax
from jax.sharding import PartitionSpec as P

FF = 16384


tanh_scale = 0.7978845608
cubic_term = 0.044715


def gelu_value(value):
    inner = tanh_scale * (value + cubic_term * value * value * value)
    return 0.5 * value * (1.0 + jnp.tanh(inner))


def gelu_slope(value):
    tangent = jnp.tanh(tanh_scale * (value + cubic_term * value * value * value))
    return 0.5 * (1.0 + tangent) + 0.5 * value * (1.0 - tangent * tangent) * tanh_scale * (
        1.0 + 3.0 * cubic_term * value * value
    )


def arrange(stored_units):
    local_width = stored_units.shape[0]
    band_ids = (
        (stored_units >= FF // 8).astype(jnp.int32)
        + (stored_units >= FF // 4).astype(jnp.int32)
        + (stored_units >= FF // 2).astype(jnp.int32)
    )
    ranking = jnp.argsort(band_ids * local_width + jnp.arange(local_width, dtype=jnp.int32))
    return (ranking, jnp.argsort(ranking))


def band_limits(local_width):
    eighth = local_width // 8
    return [(0, eighth), (eighth, 2 * eighth), (2 * eighth, 4 * eighth), (4 * eighth, local_width)]


def per_device(features, w_in, w_out, unit_order, cotangents):
    local_width = unit_order.shape[0]
    limits = band_limits(local_width)
    ranking, inverse = arrange(unit_order)
    in_columns = jnp.take(w_in, ranking, axis=1)
    out_rows = jnp.take(w_out, ranking, axis=0)
    full_x = lax.all_gather(features, "mp", axis=1, tiled=True)
    token_count = full_x.shape[0]
    full_in, full_out = (
        lax.all_gather(in_columns, "dp", axis=0, tiled=True),
        lax.all_gather(out_rows, "dp", axis=1, tiled=True),
    )
    pre = jnp.dot(full_x, full_in, preferred_element_type=jnp.float32)
    hidden = gelu_value(pre).astype(jnp.bfloat16)
    full_cot = lax.all_gather(cotangents, "mp", axis=2, tiled=True)
    combined = jnp.cumsum(full_cot.astype(jnp.float32)[::-1], axis=0)[::-1].astype(jnp.bfloat16)
    nested = []
    acc = jnp.zeros((token_count, full_out.shape[1]), jnp.float32)
    for project_lo, project_hi in limits:
        acc = acc + jnp.dot(
            hidden[:, project_lo:project_hi],
            full_out[project_lo:project_hi],
            preferred_element_type=jnp.float32,
        )
        nested.append(acc)
    out_terms = jnp.stack(nested)
    outputs = lax.psum_scatter(
        out_terms.astype(jnp.bfloat16), "mp", scatter_dimension=2, tiled=True
    )

    def add_grad_hidden(weight_piece):
        terms = [
            lax.dot_general(
                combined[level],
                weight_piece[lo:hi],
                (((1,), (1,)), ((), ())),
                preferred_element_type=jnp.float32,
            )
            for level, (lo, hi) in enumerate(limits)
        ]
        return jnp.concatenate(terms, axis=1)

    grad_hidden = add_grad_hidden(full_out)
    grad_pre = (grad_hidden * gelu_slope(pre)).astype(jnp.bfloat16)
    dx_terms = lax.dot_general(
        grad_pre, full_in, (((1,), (1,)), ((), ())), preferred_element_type=jnp.float32
    )
    grad_features = lax.psum_scatter(
        dx_terms.astype(jnp.bfloat16), "mp", scatter_dimension=1, tiled=True
    )
    grad_in_part = lax.dot_general(
        full_x, grad_pre, (((0,), (0,)), ((), ())), preferred_element_type=jnp.float32
    )
    grad_out_part = jnp.concatenate(
        [
            lax.dot_general(
                hidden[:, lo:hi],
                combined[level],
                (((0,), (0,)), ((), ())),
                preferred_element_type=jnp.float32,
            )
            for level, (lo, hi) in enumerate(limits)
        ],
        axis=0,
    )
    grad_in_sum, grad_out_sum = (
        lax.psum_scatter(
            grad_in_part.astype(jnp.bfloat16), "dp", scatter_dimension=0, tiled=True
        ).astype(jnp.float32),
        lax.psum_scatter(
            grad_out_part.astype(jnp.bfloat16), "dp", scatter_dimension=1, tiled=True
        ).astype(jnp.float32),
    )
    grad_in = jnp.take(grad_in_sum.astype(jnp.bfloat16), inverse, axis=1)
    grad_out = jnp.take(grad_out_sum.astype(jnp.bfloat16), inverse, axis=0)
    return (outputs, grad_features, grad_in, grad_out)


def solution(mesh):
    placed = (P("dp", "mp"), P("dp", "mp"), P("mp", "dp"), P("mp"), P(None, "dp", "mp"))
    return jax.shard_map(
        per_device,
        mesh=mesh,
        in_specs=placed,
        out_specs=(P(None, "dp", "mp"), P("dp", "mp"), P("dp", "mp"), P("mp", "dp")),
        check_vma=False,
    )
```

profile of v0, /device:TPU:1, one launch (start us, length us, event | category | flops | bytes accessed | tf_op | source)
XLA Modules:
  0.0 556.7 jit_solution(12127224745069479167)
XLA Ops:
  9.8 4.4 sort.31
  14.2 3.2 gather_fusion
  17.4 3.2 gather_fusion.1
  23.0 40.4 %all-gather.7.cloned.1.call-done = bf16[384,2048]{1,0:T(8,128)(2,1)} async-done(((bf16[384,128]{1,0:T(8,128)(2,1)}), bf16[384,2048]{1,0:T(8,128)(2,1)}) %all-gather.7.cloned.1.call-update) | async-done | bytes 1572880 | tf_op jit(solution)/shard_map/all_gather | solution.py:47
  63.4 52.8 %all-gather.5.cloned.1.call-done = bf16[2048,1024]{0,1:T(8,128)(2,1)} async-done(((bf16[128,1024]{0,1:T(8,128)(2,1)}), bf16[2048,1024]{0,1:T(8,128)(2,1)}) %all-gather.5.cloned.1.call-update) | async-done | bytes 4194320 | tf_op jit(solution)/shard_map/all_gather | solution.py:50
  116.3 6.4 %multiply_convert_fusion = (bf16[384,1024]{0,1:T(8,128)(2,1)S(1)}, f32[1024,384]{1,0:T(8,128)}) fusion(bf16[2048,1024]{0,1:T(8,128)(2,1)} %all-gather.5.cloned.1.call-done, bf16[384,2048]{1,0:T(8,128)(2,1)} %all-gather.7.cloned.1.call-done), kind=kOutput, calls=%fused_computation.37 | convolution fusion | flops 1614151680 | bytes 8126464 | tf_op jit(solution)/shard_map/dot_general | solution.py:53
  122.6 66.1 %all-gather.11.cloned.1.call-done = bf16[4,384,2048]{2,1,0:T(8,128)(2,1)} async-done(((bf16[4,384,128]{2,1,0:T(8,128)(2,1)}), bf16[4,384,2048]{2,1,0:T(8,128)(2,1)}) %all-gather.11.cloned.1.call-update) | async-done | bytes 6291472 | tf_op jit(solution)/shard_map/all_gather | solution.py:55
  188.7 8.8 %rev.6 = f32[4,384,2048]{2,1,0:T(8,128)} reverse(bf16[4,384,2048]{2,1,0:T(8,128)(2,1)} %all-gather.11.cloned.1.call-done), dimensions={0} | reverse | bytes 18874368 | tf_op jit(solution)/shard_map/rev | solution.py:56
  197.6 7.8 %fusion.33 = bf16[4,384,2048]{2,1,0:T(8,128)(2,1)} fusion(f32[4,384,2048]{2,1,0:T(8,128)} %rev.6), kind=kOutput, calls=%fused_computation.67 | output fusion | flops 9437184 | bytes 18874368 | tf_op jit(solution)/shard_map/jit(cumsum)/reduce_window_sum | solution.py:56
  205.4 6.6 %rev.9 = bf16[4,384,2048]{2,1,0:T(8,128)(2,1)} reverse(bf16[4,384,2048]{2,1,0:T(8,128)(2,1)} %fusion.33), dimensions={0} | reverse | bytes 12582912 | tf_op jit(solution)/shard_map/rev | solution.py:56
  211.9 29.1 %all-gather.9.cloned.1.call-done = bf16[1024,2048]{1,0:T(8,128)(2,1)} async-done(((bf16[1024,128]{1,0:T(8,128)(2,1)}), bf16[1024,2048]{1,0:T(8,128)(2,1)}) %all-gather.9.cloned.1.call-update) | async-done | bytes 4194320 | tf_op jit(solution)/shard_map/all_gather | solution.py:51
  241.1 3.5 fusion.1
  266.1 6.4 %copy.22 = bf16[1024,2048]{0,1:T(8,128)(2,1)} copy(bf16[1024,2048]{1,0:T(8,128)(2,1)} %pad_maximum_fusion.1) | data formatting | bytes 8388608
  274.0 6.5 %convert_bitcast_fusion = bf16[2048,1024]{0,1:T(8,128)(2,1)} fusion(bf16[384,2048]{1,0:T(8,128)(2,1)S(1)} %copy-done.5, f32[384,512]{0,1:T(8,128)} %copy-done.6, f32[384,256]{0,1:T(8,128)S(1)} %fusion.13, f32[384,128]{0,1:T(8,128)S(1)} %fusion.12, f32[384,128]{0,1:T(8,128)S(1)} %fusion.11, f32[1024,384]{1,0:T(8,128)} %get-tuple-element.23), kind=kOutput, calls=%fused_computation.7 | convolution fusion | flops 1621360640 | bytes 8912896 | tf_op jit(solution)/shard_map/dot_general | solution.py:91
  280.4 6.4 %copy.20 = bf16[2048,1024]{1,0:T(8,128)(2,1)} copy(bf16[2048,1024]{0,1:T(8,128)(2,1)} %convert_bitcast_fusion) | data formatting | bytes 8388608
  296.5 10.8 %copy.16 = bf16[4,384,2048]{1,0,2:T(4,128)(2,1)} copy(bf16[4,384,2048]{2,1,0:T(8,128)(2,1)} %pad_maximum_fusion) | data formatting | bytes 12582912
  307.3 6.6 %copy.24 = bf16[256,8,4,384]{3,1,2,0:T(8,128)(2,1)} copy(bf16[256,8,4,384]{3,2,1,0:T(4,128)(2,1)} %bitcast.59) | data formatting | bytes 12582912
  314.0 4.4 sort.32
  318.3 12.1 %reduce-scatter.15.cloned.1.call-done = bf16[128,384]{1,0:T(8,128)(2,1)} async-done(((bf16[2048,384]{1,0:T(8,128)(2,1)}), bf16[128,384]{1,0:T(8,128)(2,1)}) %reduce-scatter.15.cloned.1.call-update) | async-done | bytes 98320
  332.0 61.4 %reduce-scatter.19.cloned.1.call-done = bf16[128,1024]{1,0:T(8,128)(2,1)} async-done(((bf16[2048,1024]{1,0:T(8,128)(2,1)}), bf16[128,1024]{1,0:T(8,128)(2,1)}) %reduce-scatter.19.cloned.1.call-update) | async-done | bytes 262160
  394.6 62.6 %reduce-scatter.17.cloned.1.call-done = bf16[128,1024]{1,0:T(8,128)(2,1)} async-done(((bf16[2048,1024]{1,0:T(8,128)(2,1)}), bf16[128,1024]{1,0:T(8,128)(2,1)}) %reduce-scatter.17.cloned.1.call-update) | async-done | bytes 262160
  458.3 3.2 gather_fusion.2
  461.5 3.2 gather_fusion.3
  466.5 81.3 %reduce-scatter.13.cloned.1.call-done = bf16[128,1536]{1,0:T(8,128)(2,1)} async-done(((bf16[2048,1536]{1,0:T(8,128)(2,1)}), bf16[128,1536]{1,0:T(8,128)(2,1)}) %reduce-scatter.13.cloned.1.call-update) | async-done | bytes 393232
  (65 shorter events, 45.2 us)
Async XLA Ops:
  7.2 10.2 %copy-start = (bf16[1024,128]{1,0:T(8,128)(2,1)S(1)}, bf16[1024,128]{1,0:T(8,128)(2,1)}, u32[]{:S(2)}) copy-start(bf16[1024,128]{1,0:T(8,128)(2,1)} %param.11) | copy-start | bytes 786436
  7.2 56.2 %all-gather.7.cloned.1.call-start = ((), (), s32[]{:S(2)}) async-start(), calls=%async_computation.5 | async-start | bytes 1671168 | tf_op jit(solution)/shard_map/all_gather | solution.py:47
  7.9 108.4 %all-gather.5.cloned.1.call-start = ((), (), s32[]{:S(2)}) async-start(), calls=%async_computation.4 | async-start | bytes 4456448 | tf_op jit(solution)/shard_map/all_gather | solution.py:50
  21.6 167.1 %all-gather.11.cloned.1.call-start = ((), (), s32[]{:S(2)}) async-start(), calls=%async_computation.7 | async-start | bytes 6684672 | tf_op jit(solution)/shard_map/all_gather | solution.py:55
  22.4 218.7 %all-gather.9.cloned.1.call-start = ((), (), s32[]{:S(2)}) async-start(), calls=%async_computation.6 | async-start | bytes 4456448 | tf_op jit(solution)/shard_map/all_gather | solution.py:51
  22.9 307.5 %reduce-scatter.15.cloned.1.call-start = ((), (), s32[]{:S(2)}) async-start(), calls=%async_computation.9 | async-start | bytes 1671168
  241.1 3.9 copy-start.2
  245.0 5.8 %copy-start.6 = (f32[384,512]{0,1:T(8,128)}, f32[384,512]{0,1:T(8,128)S(1)}, u32[]{:S(2)}) copy-start(f32[384,512]{0,1:T(8,128)S(1)} %fusion.1) | copy-start | bytes 2359300
  247.2 3.6 copy-start.4
  249.0 1.8 copy-start.7
  255.1 138.4 %reduce-scatter.19.cloned.1.call-start = ((), (), s32[]{:S(2)}) async-start(), calls=%async_computation.11 | async-start | bytes 4456448
  272.6 1.4 copy-start.5
  272.6 184.6 %reduce-scatter.17.cloned.1.call-start = ((), (), s32[]{:S(2)}) async-start(), calls=%async_computation.10 | async-start | bytes 4456448
  286.9 260.9 %reduce-scatter.13.cloned.1.call-start = ((), (), s32[]{:S(2)}) async-start(), calls=%async_computation.8 | async-start | bytes 6684672
  288.5 2.4 copy-start.3
  461.5 88.4 %copy-start.1 = (bf16[1024,128]{1,0:T(8,128)(2,1)S(1)}, bf16[1024,128]{1,0:T(8,128)(2,1)}, u32[]{:S(2)}) copy-start(bf16[1024,128]{1,0:T(8,128)(2,1)} %param.11) | copy-start | bytes 786436
Sparse Core Ops, SparseCore 0:
  10.4 52.9 all-gather.6
  65.7 50.4 all-gather.4
  118.7 70.0 all-gather.10
  190.9 50.1 all-gather.8
  255.2 75.1 reduce-scatter.14
  332.8 60.5 reduce-scatter.18
  396.0 61.1 reduce-scatter.16
  460.9 86.9 reduce-scatter.12
where the time goes:
time: 558 us; the launch traced here: 557 us
  waiting for transfers between devices  408 us (73%)
  local copies, waits for them, and re-layouts  70.3 us (13%)
  matrix products  38.3 us (7%)
  other arithmetic  25.4 us (5%)
  between operations  14.4 us (3%)
    unnamed x12, waiting for transfers between devices  219 us
    all_gather x1, waiting for transfers between devices, per_device(): full_cot = lax.all_gather(cotangents, 'mp', axis=2, tiled=True)  66.1 us
    all_gather x1, waiting for transfers between devices, per_device(): lax.all_gather(in_columns, 'dp', axis=0, tiled=True)  52.8 us
    unnamed x28, local copies, waits for them, and re-layouts  42.1 us
    all_gather x1, waiting for transfers between devices, per_device(): full_x = lax.all_gather(features, 'mp', axis=1, tiled=True)  40.4 us
    all_gather x1, waiting for transfers between devices, per_device(): lax.all_gather(out_rows, 'dp', axis=1, tiled=True)  29.1 us
  transfers between devices with their start and end apart: 8, of which 8 were waited for; matrix products, arithmetic and copies ran while one was open for 21% of the time, Pallas kernels for 0%

commit v1 on v0

v1 whole, which is shorter than its diff:
```python
import functools

import jax
import jax.numpy as jnp
from jax import lax
from jax.experimental import pallas as pl
from jax.experimental.pallas import tpu as pltpu
from jax.sharding import Mesh, PartitionSpec as P

FF = 16384
MP = 16
Z = 8
SHARE = 64
HALF = SHARE // 2
UNITS = MP * HALF
LAST_OF_BAND = (1, 3, 7, 15)

tanh_scale = 0.7978845608
cubic_term = 0.044715

F32 = jnp.float32
BF16 = jnp.bfloat16
MXN = (((1,), (1,)), ((), ()))
TN = (((0,), (0,)), ((), ()))


def params(mib=48):
    return pltpu.CompilerParams(vmem_limit_bytes=mib << 20)


def one_hot(places):
    size = places.shape[1]
    return (lax.broadcasted_iota(jnp.int32, (size, size), 0) == places).astype(BF16)


def sort_kernel(core_ref, units_ref, w_in_ref, w_out_ref, own_ref, other_ref, places_ref):
    units = units_ref[...]
    size = units.shape[1]
    band = (
        (units >= FF // 8).astype(jnp.int32)
        + (units >= FF // 4).astype(jnp.int32)
        + (units >= FF // 2).astype(jnp.int32)
    )
    rows = lax.broadcasted_iota(jnp.int32, (8, size), 0)
    member = rows == band
    before = (
        lax.broadcasted_iota(jnp.int32, (size, size), 0)
        < lax.broadcasted_iota(jnp.int32, (size, size), 1)
    ).astype(BF16)
    count = jnp.dot(member.astype(BF16), before, preferred_element_type=F32)
    base = jnp.where(rows == 0, 0, jnp.where(rows == 1, size // 8, jnp.where(rows == 2, size // 4, size // 2)))
    rank = jnp.sum(jnp.where(member, count + base.astype(F32), 0.0), axis=0, keepdims=True).astype(jnp.int32)
    dest = rank // SHARE
    within = rank % SHARE
    half = within // HALF
    places = jnp.where(half == core_ref[0], 0, UNITS) + dest * HALF + within % HALF
    places_ref[...] = places
    picks = one_hot(places)
    rows_in = lax.dot_general(picks, w_in_ref[...], MXN, preferred_element_type=F32).astype(BF16)
    rows_out = jnp.dot(picks, w_out_ref[...], preferred_element_type=F32).astype(BF16)
    for k in range(MP):
        lo = k * HALF
        own_ref[k, 0] = rows_in[lo : lo + HALF]
        own_ref[k, 1] = rows_out[lo : lo + HALF]
        other_ref[k, 0] = rows_in[UNITS + lo : UNITS + lo + HALF]
        other_ref[k, 1] = rows_out[UNITS + lo : UNITS + lo + HALF]


def unsort_kernel(places_ref, own_ref, other_ref, grad_in_ref, grad_out_ref):
    picks = one_hot(places_ref[...])

    def rows(i):
        return jnp.concatenate([own_ref[k, i] for k in range(MP)] + [other_ref[k, i] for k in range(MP)], axis=0)

    grad_in_ref[...] = lax.dot_general(rows(0), picks, TN, preferred_element_type=F32).astype(BF16)
    grad_out_ref[...] = lax.dot_general(rows(1), picks, TN, preferred_element_type=F32).T.astype(BF16)


def tokens_kernel(x_ref, cot_ref, send_ref):
    x = x_ref[...]
    total = cot_ref[3].astype(F32)
    combined = [None] * 4
    combined[3] = cot_ref[3]
    for b in (2, 1, 0):
        total = total + cot_ref[b].astype(F32)
        combined[b] = total.astype(BF16)
    first = 0
    for b, last in enumerate(LAST_OF_BAND):
        for k in range(first, last + 1):
            send_ref[k, 0] = x
            send_ref[k, 1] = combined[b]
        first = last + 1


def grads_kernel(
    own_ref, peer_ref, weights_ref, grads_ref, hidden_ref, grad_pre_ref,
    x_ref, comb_ref, in_ref, out_ref, part_ref, hid_ref, gpre_ref, token_sem, weight_sem, grad_sem, keep_sem,
):
    count = own_ref.shape[1]
    loads = []
    for half, ref in enumerate((own_ref, peer_ref)):
        for i, to in enumerate((x_ref, comb_ref)):
            loads.append(
                pltpu.make_async_copy(ref.at[i], to.at[pl.ds(half * count, count)], token_sem.at[2 * half + i])
            )
    width = weights_ref.shape[-1]
    for z in range(Z):
        for i, to in enumerate((in_ref, out_ref)):
            loads.append(
                pltpu.make_async_copy(
                    weights_ref.at[z, :, i], to.at[:, :, pl.ds(z * width, width)], weight_sem.at[2 * z + i]
                )
            )
    for load in loads:
        load.start()
    for load in loads:
        load.wait()
    full = in_ref.shape[-1]
    w_in = in_ref[...].reshape(UNITS, full)
    w_out = out_ref[...].reshape(UNITS, full)
    step = 256
    for lo in range(0, 2 * count, step):
        pre = lax.dot_general(w_in, x_ref[lo : lo + step], MXN, preferred_element_type=F32)
        back = lax.dot_general(w_out, comb_ref[lo : lo + step], MXN, preferred_element_type=F32)
        square = pre * pre
        tangent = jnp.tanh(tanh_scale * (pre + cubic_term * square * pre))
        hid_ref[:, lo : lo + step] = (0.5 * pre * (1.0 + tangent)).astype(BF16)
        slope = 0.5 * (1.0 + tangent) + 0.5 * pre * (1.0 - tangent * tangent) * tanh_scale * (
            1.0 + 3.0 * cubic_term * square
        )
        gpre_ref[:, lo : lo + step] = (back * slope).astype(BF16)
    keeps = [
        pltpu.make_async_copy(hid_ref, hidden_ref, keep_sem.at[0]),
        pltpu.make_async_copy(gpre_ref, grad_pre_ref, keep_sem.at[1]),
    ]
    for keep in keeps:
        keep.start()
    stores = []
    for z in range(Z):
        lo = z * width
        grad_in = jnp.dot(gpre_ref[...], x_ref[:, lo : lo + width], preferred_element_type=F32)
        grad_out = jnp.dot(hid_ref[...], comb_ref[:, lo : lo + width], preferred_element_type=F32)
        part_ref[z, :, 0] = grad_in.astype(BF16).reshape(MP, HALF, width)
        part_ref[z, :, 1] = grad_out.astype(BF16).reshape(MP, HALF, width)
        store = pltpu.make_async_copy(part_ref.at[z], grads_ref.at[z], grad_sem.at[z])
        store.start()
        stores.append(store)
    for copy in keeps + stores:
        copy.wait()


def project_kernel(hidden_ref, grad_pre_ref, weights_ref, own_ref, other_ref, hid_ref, gpre_ref):
    @pl.when(pl.program_id(0) == 0)
    def _():
        hid_ref[...] = hidden_ref[...].T
        gpre_ref[...] = grad_pre_ref[...].T

    width = weights_ref.shape[-1]
    w_in = weights_ref[0, :, 0].reshape(UNITS, width)
    w_out = weights_ref[0, :, 1].reshape(UNITS, width)
    for i, (left, right) in enumerate(((hid_ref, w_out), (gpre_ref, w_in))):
        whole = jnp.dot(left[...], right, preferred_element_type=F32).astype(BF16)
        count = whole.shape[0] // 2
        part = width // 2
        for side in range(2):
            own_ref[side, i] = whole[:count, side * part : (side + 1) * part]
            other_ref[side, i] = whole[count:, side * part : (side + 1) * part]


def sums_kernel(got_ref, outputs_ref, dx_ref):
    total = jnp.zeros(dx_ref.shape, F32)
    for k in range(MP):
        total = total + got_ref[k, 0].astype(F32)
        if k in LAST_OF_BAND:
            outputs_ref[LAST_OF_BAND.index(k)] = total.astype(BF16)
    total = jnp.zeros(dx_ref.shape, F32)
    for k in range(MP):
        total = total + got_ref[k, 1].astype(F32)
    dx_ref[...] = total.astype(BF16)


ANY = pl.BlockSpec(memory_space=pl.ANY)
VMEM = pl.BlockSpec(memory_space=pltpu.VMEM)
SMEM = pl.BlockSpec(memory_space=pltpu.SMEM)


def struct(*shape, dtype=BF16):
    return jax.ShapeDtypeStruct(shape, dtype)


def to_other_core(value):
    return lax.ppermute(value, "core", [(0, 1), (1, 0)])


def exchange(value):
    return lax.all_to_all(value, ("y", "x"), 0, 0, tiled=True)


def after(value, earlier):
    return lax.optimization_barrier((value, earlier))[0]


def per_device(features, w_in, w_out, unit_order, cotangents):
    core = lax.axis_index("core")
    count, part = features.shape
    units = unit_order.shape[0]
    width = 2 * part
    full = MP * part
    own, other, places = pl.pallas_call(
        sort_kernel,
        out_shape=(
            struct(MP, 2, HALF, part),
            struct(MP, 2, HALF, part),
            struct(1, units, dtype=jnp.int32),
        ),
        in_specs=[SMEM, VMEM, VMEM, VMEM],
        out_specs=(VMEM, VMEM, VMEM),
        compiler_params=params(),
        name="sort_units",
    )(core.reshape(1), unit_order.reshape(1, units), w_in, w_out)
    got = to_other_core(other)
    both = jnp.where(core == 0, jnp.concatenate([own, got], axis=3), jnp.concatenate([got, own], axis=3))
    mine = exchange(both)
    weights = lax.all_gather(mine.reshape(2 * UNITS, width), "z", axis=0, tiled=True)
    weights = weights.reshape(Z, MP, 2, HALF, width)

    send = pl.pallas_call(
        tokens_kernel,
        out_shape=struct(MP, 2, count, part),
        in_specs=[VMEM, VMEM],
        out_specs=VMEM,
        compiler_params=params(),
        name="combine_cotangents",
    )(features, cotangents)
    tokens = exchange(after(send, mine))
    tokens = tokens.transpose(1, 2, 0, 3).reshape(2, count, full)
    peer_tokens = to_other_core(tokens)

    grads, hidden, grad_pre = pl.pallas_call(
        grads_kernel,
        out_shape=(
            struct(Z, MP, 2, HALF, width),
            struct(UNITS, 2 * count),
            struct(UNITS, 2 * count),
        ),
        in_specs=[ANY] * 3,
        out_specs=(ANY,) * 3,
        scratch_shapes=[
            pltpu.VMEM((2 * count, full), BF16),
            pltpu.VMEM((2 * count, full), BF16),
            pltpu.VMEM((MP, HALF, full), BF16),
            pltpu.VMEM((MP, HALF, full), BF16),
            pltpu.VMEM((Z, MP, 2, HALF, width), BF16),
            pltpu.VMEM((UNITS, 2 * count), BF16),
            pltpu.VMEM((UNITS, 2 * count), BF16),
            pltpu.SemaphoreType.DMA((4,)),
            pltpu.SemaphoreType.DMA((2 * Z,)),
            pltpu.SemaphoreType.DMA((Z,)),
            pltpu.SemaphoreType.DMA((2,)),
        ],
        compiler_params=params(),
        cost_estimate=pl.CostEstimate(flops=8 * UNITS * 2 * count * full, bytes_accessed=16 << 20, transcendentals=UNITS * 2 * count),
        name="hidden_and_weight_grads",
    )(tokens, peer_tokens, weights)
    summed = lax.psum_scatter(grads.reshape(Z * 2 * UNITS, width), "z", scatter_dimension=0, tiled=True)
    summed = summed.reshape(MP, 2, HALF, width)

    out_own, out_other = pl.pallas_call(
        project_kernel,
        grid=(Z,),
        out_shape=(struct(MP, 2, count, part), struct(MP, 2, count, part)),
        in_specs=[
            pl.BlockSpec((UNITS, 2 * count), lambda z: (0, 0)),
            pl.BlockSpec((UNITS, 2 * count), lambda z: (0, 0)),
            pl.BlockSpec((1, MP, 2, HALF, width), lambda z: (z, 0, 0, 0, 0)),
        ],
        out_specs=(
            pl.BlockSpec((2, 2, count, part), lambda z: (z, 0, 0, 0)),
            pl.BlockSpec((2, 2, count, part), lambda z: (z, 0, 0, 0)),
        ),
        scratch_shapes=[pltpu.VMEM((2 * count, UNITS), BF16), pltpu.VMEM((2 * count, UNITS), BF16)],
        compiler_params=params(),
        cost_estimate=pl.CostEstimate(flops=4 * UNITS * 2 * count * full, bytes_accessed=12 << 20, transcendentals=0),
        name="outputs_and_feature_grads",
    )(hidden, grad_pre, weights)
    out_peer = to_other_core(out_other)
    out_sum = (out_own.astype(F32) + out_peer.astype(F32)).astype(BF16)
    out_got = exchange(out_sum)
    rows = 128
    outputs, grad_features = pl.pallas_call(
        sums_kernel,
        grid=(count // rows,),
        out_shape=(struct(4, count, part), struct(count, part)),
        in_specs=[pl.BlockSpec((MP, 2, rows, part), lambda t: (0, 0, t, 0))],
        out_specs=(
            pl.BlockSpec((4, rows, part), lambda t: (0, t, 0)),
            pl.BlockSpec((rows, part), lambda t: (t, 0)),
        ),
        compiler_params=params(),
        name="sum_outputs",
    )(out_got)

    left, right = summed[..., :part], summed[..., part:]
    keep = jnp.where(core == 0, left, right)
    give = jnp.where(core == 0, right, left)
    taken = to_other_core(give)
    back = exchange(after(jnp.stack([keep, taken], axis=1), out_got))
    grad_in, grad_out = pl.pallas_call(
        unsort_kernel,
        out_shape=(struct(part, units), struct(units, part)),
        in_specs=[VMEM, VMEM, VMEM],
        out_specs=(VMEM, VMEM),
        compiler_params=params(),
        name="unsort_grads",
    )(places, back[:, 0], back[:, 1])
    return outputs, grad_features, grad_in, grad_out


def solution(mesh):
    whole = Mesh(mesh.devices.reshape(Z, 2, 4, 4), ("z", "core", "y", "x"))
    dp, mp = ("z", "core"), ("y", "x")
    return jax.shard_map(
        per_device,
        mesh=whole,
        in_specs=(P(dp, mp), P(dp, mp), P(mp, dp), P(mp), P(None, dp, mp)),
        out_specs=(P(None, dp, mp), P(dp, mp), P(dp, mp), P(mp, dp)),
        check_vma=False,
    )
```

time: 558 us -> 199 us (0.36)
  waiting for transfers between devices: 408 us -> 70 us
  local copies, waits for them, and re-layouts: 70.3 us -> 7.34 us
  blocking collectives: 0 us -> 57.4 us
  matrix products: 38.3 us -> 0 us
  Pallas kernels: 0 us -> 26.5 us
  other arithmetic: 25.4 us -> 4.91 us
  starting transfers between devices: 0.5 us -> 17.9 us
    unnamed x12 -> x2, waiting for transfers between devices: 219 us -> 0.03 us
    all_gather x4 -> x1, waiting for transfers between devices: 189 us -> 4.62 us  [per_device(): lax.all_gather(mine.reshape(2 * UNITS, width), 'z', axis=0, tiled=True)]
    all_to_all x0 -> x2, blocking collectives: none -> 57.4 us  [exchange(): return lax.all_to_all(value, ('y', 'x'), 0, 0, tiled=True)]
    dot_general x15 -> x0, matrix products: 38.3 us -> none  [the longest x4 9.25 us: add_grad_hidden(): lax.dot_general(combined[level], weight_piece[lo:hi], (((1,), (1,)), ((),...]
    unnamed x28 -> x18, local copies, waits for them, and re-layouts: 42.1 us -> 5.83 us
    reduce_scatter x0 -> x1, waiting for transfers between devices: none -> 28.4 us  [per_device(): lax.psum_scatter(grads.reshape(Z * 2 * UNITS, width), 'z', scatter_dimens...]
    pallas_call x0 -> x6, Pallas kernels: none -> 26.5 us  [the longest x1 12 us: per_device(): pl.pallas_call(grads_kernel, out_shape=(struct(Z, MP, 2, HALF, width), st...]
    all_to_all x0 -> x2, waiting for transfers between devices: none -> 23.7 us  [exchange(): return lax.all_to_all(value, ('y', 'x'), 0, 0, tiled=True)]
  transfers between devices with their start and end apart: 8 -> 8, of which waited for: 8 -> 8; matrix products, arithmetic and copies ran while one was open for 21% -> 3% of each run, Pallas kernels for 0% -> 6%
where the time goes in v1:
time: 199 us; the launch traced here: 198 us
  waiting for transfers between devices  70 us (35%)
  blocking collectives  57.4 us (29%)
  Pallas kernels  26.5 us (13%)
  starting transfers between devices  17.9 us (9%)
  between operations  14.2 us (7%)
  local copies, waits for them, and re-layouts  7.34 us (4%)
  other arithmetic  4.91 us (2%)
    all_to_all x2, blocking collectives, exchange(): return lax.all_to_all(value, ('y', 'x'), 0, 0, tiled=True)  57.4 us
    reduce_scatter x1, waiting for transfers between devices, per_device(): lax.psum_scatter(grads.reshape(Z * 2 * UNITS, width), 'z', scatter_dimens...  28.4 us
    all_to_all x2, waiting for transfers between devices, exchange(): return lax.all_to_all(value, ('y', 'x'), 0, 0, tiled=True)  23.7 us
    ppermute x4, waiting for transfers between devices, to_other_core(): return lax.ppermute(value, 'core', [(0, 1), (1, 0)])  13.2 us
    pallas_call x1, Pallas kernels, per_device(): pl.pallas_call(grads_kernel, out_shape=(struct(Z, MP, 2, HALF, width), st...  12 us
    all_to_all x2, starting transfers between devices, exchange(): return lax.all_to_all(value, ('y', 'x'), 0, 0, tiled=True)  10.8 us
    pallas_call x1, Pallas kernels, per_device(): pl.pallas_call(project_kernel, grid=(Z,), out_shape=(struct(MP, 2, count,...  8.91 us
    ppermute x4, starting transfers between devices, to_other_core(): return lax.ppermute(value, 'core', [(0, 1), (1, 0)])  7.06 us
  transfers between devices with their start and end apart: 8, of which 8 were waited for; matrix products, arithmetic and copies ran while one was open for 3% of the time, Pallas kernels for 6%

profile of v1, /device:TPU:1, one launch (start us, length us, event | category | flops | bytes accessed | tf_op | source)
XLA Modules:
  0.0 198.2 jit_solution(16205798330150841525)
XLA Ops:
  7.2 1.0 copy-done.1
  9.9 1.4 sort_units.1
  11.3 3.3 %collective-permute-start = (bf16[16,2,32,128]{3,2,1,0:T(8,128)(2,1)S(1)}, bf16[16,2,32,128]{3,2,1,0:T(8,128)(2,1)S(1)}, u32[]{:S(2)}, u32[]{:S(2)}) collective-permute-start(bf16[16,2,32,128]{3,2,1,0:T(8,128)(2,1)S(1)} %get-tuple-element.19), channel_id=1, source_target_pairs={{0,16},{16,0},{1,17},{17,1},{2,18},{18,2},{3,19},{19,3},{4,20},{20... | collective-permute-start | bytes 786440 | tf_op jit(solution)/shard_map/ppermute | solution.py:192
  14.6 1.2 collective-permute-done
  16.1 15.6 %all_to_all.20 = bf16[16,2,32,256]{3,2,1,0:T(8,128)(2,1)} all-to-all(bf16[16,2,32,256]{3,2,1,0:T(8,128)(2,1)S(1)} %maximum_select_fusion), channel_id=1, replica_groups=mesh['z'=8,'core'=2,'y'=4,'x'=4] {'y','x'}, dimensions={0} | all-to-all | bytes 1048576 | tf_op jit(solution)/shard_map/all_to_all | solution.py:196
  32.3 41.8 %all_to_all.21 = bf16[16,2,384,128]{3,2,1,0:T(8,128)(2,1)S(1)} all-to-all(bf16[16,2,384,128]{3,2,1,0:T(8,128)(2,1)S(1)} %combine_cotangents.1), channel_id=1, replica_groups=mesh['z'=8,'core'=2,'y'=4,'x'=4] {'y','x'}, dimensions={0} | all-to-all | bytes 6291456 | tf_op jit(solution)/shard_map/all_to_all | solution.py:196
  74.5 2.4 %collective-permute-start.1 = (bf16[2,384,2048]{2,1,0:T(8,128)(2,1)S(1)}, bf16[2,384,2048]{2,1,0:T(8,128)(2,1)}, u32[]{:S(2)}, u32[]{:S(2)}) collective-permute-start(bf16[2,384,2048]{2,1,0:T(8,128)(2,1)S(1)} %copy_bitcast_fusion.own_ref), channel_id=1, source_target_pairs={{0,16},{16,0},{1,17},{17,1},{2,18},{18,2},{3,19},{19,3},{4,20},{20... | collective-permute-start | bytes 9437192 | tf_op jit(solution)/shard_map/ppermute | solution.py:192
  76.9 5.4 %collective-permute-done.1.peer_ref = bf16[2,384,2048]{2,1,0:T(8,128)(2,1)} collective-permute-done((bf16[2,384,2048]{2,1,0:T(8,128)(2,1)S(1)}, bf16[2,384,2048]{2,1,0:T(8,128)(2,1)}, u32[]{:S(2)}, u32[]{:S(2)}) %collective-permute-start.1) | collective-permute-done | bytes 3145760 | tf_op jit(solution)/shard_map/ppermute | solution.py:192
  82.3 4.6 %all-gather.2.cloned.1.call-done = bf16[8192,256]{1,0:T(8,128)(2,1)} async-done(((bf16[1024,256]{1,0:T(8,128)(2,1)}), bf16[8192,256]{1,0:T(8,128)(2,1)}) %all-gather.2.cloned.1.call-update) | async-done | bytes 4194320 | tf_op jit(solution)/shard_map/all_gather | solution.py:224
  86.9 12.0 %hidden_and_weight_grads.1 = (bf16[8,16,2,32,256]{4,3,2,1,0:T(8,128)(2,1)}, bf16[512,768]{1,0:T(8,128)(2,1)S(1)}, bf16[512,768]{1,0:T(8,128)(2,1)S(1)}) custom-call(bf16[2,384,2048]{2,1,0:T(8,128)(2,1)S(1)} %copy_bitcast_fusion.own_ref, bf16[2,384,2048]{2,1,0:T(8,128)(2,1)} %collective-permute-done.1.peer_ref, bf16[8,16,2,32,256]{4,3,2,1,0:T(8,128)(2,1)} %bitcast.30), custom_call_target="tpu_custom_call" | custom-call | flops 6442450944 | bytes 16777216 | tf_op jit(solution)/shard_map/hidden_and_weight_grads/pallas_call | solution.py:239
  100.8 1.1 copy-done.6
  102.2 8.9 %outputs_and_feature_grads.1 = (bf16[16,2,384,128]{3,2,1,0:T(8,128)(2,1)S(1)}, bf16[16,2,384,128]{3,2,1,0:T(8,128)(2,1)}) custom-call(bf16[512,768]{1,0:T(8,128)(2,1)S(1)} %copy-done.6, bf16[512,768]{1,0:T(8,128)(2,1)S(1)} %copy-done.8, bf16[8,16,2,32,256]{4,3,2,1,0:T(8,128)(2,1)} %bitcast.31), custom_call_target="tpu_custom_call" | custom-call | flops 3221225472 | bytes 12582912 | tf_op jit(solution)/shard_map/outputs_and_feature_grads/pallas_call | solution.py:268
  111.7 5.5 %collective-permute-done.2 = bf16[16,2,384,128]{3,2,1,0:T(8,128)(2,1)S(1)} collective-permute-done((bf16[16,2,384,128]{3,2,1,0:T(8,128)(2,1)}, bf16[16,2,384,128]{3,2,1,0:T(8,128)(2,1)S(1)}, u32[]{:S(2)}, u32[]{:S(2)}) %collective-permute-start.2) | collective-permute-done | bytes 3145760 | tf_op jit(solution)/shard_map/ppermute | solution.py:192
  117.2 2.7 %add_convert_fusion = bf16[16,2,384,128]{3,2,1,0:T(8,128)(2,1)} fusion(bf16[16,2,384,128]{3,2,1,0:T(8,128)(2,1)S(1)} %collective-permute-done.2, bf16[16,2,384,128]{3,2,1,0:T(8,128)(2,1)S(1)} %get-tuple-element.23), kind=kLoop, calls=%fused_computation | loop fusion | flops 6291456 | bytes 9437184 | tf_op jit(solution)/shard_map/convert_element_type | solution.py:287
  120.0 6.5 %all-to-all-start.2 = ((bf16[16,2,384,128]{3,2,1,0:T(8,128)(2,1)}), bf16[16,2,384,128]{3,2,1,0:T(8,128)(2,1)S(1)}, u32[]{:S(2)}, u32[]{:S(2)}) async-start(bf16[16,2,384,128]{3,2,1,0:T(8,128)(2,1)} %add_convert_fusion), calls=%async_computation.2 | async-start | bytes 6291456 | tf_op jit(solution)/shard_map/all_to_all | solution.py:196
  126.5 28.4 %reduce-scatter.2.cloned.1.call-done = bf16[1024,256]{1,0:T(8,128)(2,1)} async-done(((bf16[8192,256]{1,0:T(8,128)(2,1)}), bf16[1024,256]{1,0:T(8,128)(2,1)}) %reduce-scatter.2.cloned.1.call-update) | async-done | bytes 524304 | tf_op jit(solution)/shard_map/reduce_scatter | solution.py:265
  154.9 1.1 select_bitcast_fusion
  156.7 1.2 collective-permute-done.3
  158.7 15.4 %all-to-all-done.2.got_ref = bf16[16,2,384,128]{3,2,1,0:T(8,128)(2,1)S(1)} async-done(((bf16[16,2,384,128]{3,2,1,0:T(8,128)(2,1)}), bf16[16,2,384,128]{3,2,1,0:T(8,128)(2,1)S(1)}, u32[]{:S(2)}, u32[]{:S(2)}) %all-to-all-start.2) | async-done | bytes 3145760 | tf_op jit(solution)/shard_map/all_to_all | solution.py:196
  174.1 4.2 %all-to-all-start.3 = ((bf16[16,2,2,32,128]{4,3,2,1,0:T(8,128)(2,1)}), bf16[16,2,2,32,128]{4,3,2,1,0:T(8,128)(2,1)}, u32[]{:S(2)}, u32[]{:S(2)}) async-start(bf16[16,2,2,32,128]{4,3,2,1,0:T(8,128)(2,1)} %pad_maximum_fusion), calls=%async_computation.4 | async-start | bytes 1048576 | tf_op jit(solution)/shard_map/all_to_all | solution.py:196
  178.4 1.8 sum_outputs.1
  180.1 8.3 %all-to-all-done.3 = bf16[16,2,2,32,128]{4,3,2,1,0:T(8,128)(2,1)} async-done(((bf16[16,2,2,32,128]{4,3,2,1,0:T(8,128)(2,1)}), bf16[16,2,2,32,128]{4,3,2,1,0:T(8,128)(2,1)}, u32[]{:S(2)}, u32[]{:S(2)}) %all-to-all-start.3) | async-done | bytes 524320 | tf_op jit(solution)/shard_map/all_to_all | solution.py:196
  188.5 1.1 slice_bitcast_fusion
  189.5 1.8 unsort_grads.1
  (26 shorter events, 7.3 us)
Async XLA Ops:
  7.2 24.6 %copy-start = (bf16[4,384,128]{2,1,0:T(8,128)(2,1)S(1)}, bf16[4,384,128]{2,1,0:T(8,128)(2,1)}, u32[]{:S(2)}) copy-start(bf16[4,384,128]{2,1,0:T(8,128)(2,1)} %cot_ref.1) | copy-start | bytes 1179652
  7.2 79.7 %all-gather.2.cloned.1.call-start = ((), (), s32[]{:S(2)}) async-start(), calls=%async_computation.5 | async-start | bytes 4718592 | tf_op jit(solution)/shard_map/all_gather | solution.py:224
  7.2 1.0 copy-start.1
  8.2 0.9 copy-start.2
  9.2 0.7 copy-start.4
  9.9 21.9 %copy-start.3 = (bf16[384,128]{1,0:T(8,128)(2,1)S(1)}, bf16[384,128]{1,0:T(8,128)(2,1)}, u32[]{:S(2)}) copy-start(bf16[384,128]{1,0:T(8,128)(2,1)} %x_ref.1) | copy-start | bytes 294916
  11.3 4.5 %collective-permute-start = (bf16[16,2,32,128]{3,2,1,0:T(8,128)(2,1)S(1)}, bf16[16,2,32,128]{3,2,1,0:T(8,128)(2,1)S(1)}, u32[]{:S(2)}, u32[]{:S(2)}) collective-permute-start(bf16[16,2,32,128]{3,2,1,0:T(8,128)(2,1)S(1)} %get-tuple-element.19), channel_id=1, source_target_pairs={{0,16},{16,0},{1,17},{17,1},{2,18},{18,2},{3,19},{19,3},{4,20},{20... | collective-permute-start | bytes 786440 | tf_op jit(solution)/shard_map/ppermute | solution.py:192
  31.7 123.2 %reduce-scatter.2.cloned.1.call-start = ((), (), s32[]{:S(2)}) async-start(), calls=%async_computation.6 | async-start | bytes 4718592 | tf_op jit(solution)/shard_map/reduce_scatter | solution.py:265
  74.5 7.8 %collective-permute-start.1 = (bf16[2,384,2048]{2,1,0:T(8,128)(2,1)S(1)}, bf16[2,384,2048]{2,1,0:T(8,128)(2,1)}, u32[]{:S(2)}, u32[]{:S(2)}) collective-permute-start(bf16[2,384,2048]{2,1,0:T(8,128)(2,1)S(1)} %copy_bitcast_fusion.own_ref), channel_id=1, source_target_pairs={{0,16},{16,0},{1,17},{17,1},{2,18},{18,2},{3,19},{19,3},{4,20},{20... | collective-permute-start | bytes 9437192 | tf_op jit(solution)/shard_map/ppermute | solution.py:192
  98.9 1.0 copy-start.5
  99.9 0.9 copy-start.7
  100.8 1.1 copy-start.6
  100.8 1.4 copy-start.8
  111.1 6.2 %collective-permute-start.2 = (bf16[16,2,384,128]{3,2,1,0:T(8,128)(2,1)}, bf16[16,2,384,128]{3,2,1,0:T(8,128)(2,1)S(1)}, u32[]{:S(2)}, u32[]{:S(2)}) collective-permute-start(bf16[16,2,384,128]{3,2,1,0:T(8,128)(2,1)} %get-tuple-element.24), channel_id=1, source_target_pairs={{0,16},{16,0},{1,17},{17,1},{2,18},{18,2},{3,19},{19,3},{4,20},{20... | collective-permute-start | bytes 9437192 | tf_op jit(solution)/shard_map/ppermute | solution.py:192
  120.0 54.1 %all-to-all-start.2 = ((bf16[16,2,384,128]{3,2,1,0:T(8,128)(2,1)}), bf16[16,2,384,128]{3,2,1,0:T(8,128)(2,1)S(1)}, u32[]{:S(2)}, u32[]{:S(2)}) async-start(bf16[16,2,384,128]{3,2,1,0:T(8,128)(2,1)} %add_convert_fusion), calls=%async_computation.2 | async-start | bytes 6291456 | tf_op jit(solution)/shard_map/all_to_all | solution.py:196
  156.0 1.9 collective-permute-start.3
  174.1 14.4 %all-to-all-start.3 = ((bf16[16,2,2,32,128]{4,3,2,1,0:T(8,128)(2,1)}), bf16[16,2,2,32,128]{4,3,2,1,0:T(8,128)(2,1)}, u32[]{:S(2)}, u32[]{:S(2)}) async-start(bf16[16,2,2,32,128]{4,3,2,1,0:T(8,128)(2,1)} %pad_maximum_fusion), calls=%async_computation.4 | async-start | bytes 1048576 | tf_op jit(solution)/shard_map/all_to_all | solution.py:196
Sparse Core Ops, SparseCore 0:
  31.8 54.9 all-gather.1
  100.9 53.9 reduce-scatter.1

commit v2 on v1

v2 whole, which is shorter than its diff:
```python
import functools

import jax
import jax.numpy as jnp
from jax import lax
from jax.experimental import pallas as pl
from jax.experimental.pallas import tpu as pltpu
from jax.sharding import Mesh, PartitionSpec as P

FF = 16384
MP = 16
Z = 8
SHARE = 64
HALF = SHARE // 2
UNITS = MP * HALF
LAST_OF_BAND = (1, 3, 7, 15)

tanh_scale = 0.7978845608
cubic_term = 0.044715

F32 = jnp.float32
BF16 = jnp.bfloat16
MXN = (((1,), (1,)), ((), ()))
TN = (((0,), (0,)), ((), ()))


def params(mib=24):
    return pltpu.CompilerParams(vmem_limit_bytes=mib << 20)


def one_hot(places):
    size = places.shape[1]
    return (lax.broadcasted_iota(jnp.int32, (size, size), 0) == places).astype(BF16)


def sort_kernel(
    core_ref, units_ref, w_in_hbm, w_out_hbm, own_ref, other_ref, places_ref, w_in_ref, w_out_ref, load_sem
):
    loads = [
        pltpu.make_async_copy(w_in_hbm, w_in_ref, load_sem.at[0]),
        pltpu.make_async_copy(w_out_hbm, w_out_ref, load_sem.at[1]),
    ]
    for load in loads:
        load.start()
    units = units_ref[...]
    size = units.shape[1]
    band = (
        (units >= FF // 8).astype(jnp.int32)
        + (units >= FF // 4).astype(jnp.int32)
        + (units >= FF // 2).astype(jnp.int32)
    )
    rows = lax.broadcasted_iota(jnp.int32, (8, size), 0)
    member = rows == band
    before = (
        lax.broadcasted_iota(jnp.int32, (size, size), 0)
        < lax.broadcasted_iota(jnp.int32, (size, size), 1)
    ).astype(BF16)
    count = jnp.dot(member.astype(BF16), before, preferred_element_type=F32)
    base = jnp.where(rows == 0, 0, jnp.where(rows == 1, size // 8, jnp.where(rows == 2, size // 4, size // 2)))
    rank = jnp.sum(jnp.where(member, count + base.astype(F32), 0.0), axis=0, keepdims=True).astype(jnp.int32)
    dest = rank // SHARE
    within = rank % SHARE
    half = within // HALF
    places = jnp.where(half == core_ref[0], 0, UNITS) + dest * HALF + within % HALF
    places_ref[...] = places
    picks = one_hot(places)
    for load in loads:
        load.wait()
    rows_in = lax.dot_general(picks, w_in_ref[...], MXN, preferred_element_type=F32).astype(BF16)
    rows_out = jnp.dot(picks, w_out_ref[...], preferred_element_type=F32).astype(BF16)
    for k in range(MP):
        lo = k * HALF
        own_ref[k, 0] = rows_in[lo : lo + HALF]
        own_ref[k, 1] = rows_out[lo : lo + HALF]
        other_ref[k, 0] = rows_in[UNITS + lo : UNITS + lo + HALF]
        other_ref[k, 1] = rows_out[UNITS + lo : UNITS + lo + HALF]


def unsort_kernel(places_ref, own_ref, other_ref, grad_in_ref, grad_out_ref):
    picks = one_hot(places_ref[...])

    def rows(i):
        return jnp.concatenate([own_ref[k, i] for k in range(MP)] + [other_ref[k, i] for k in range(MP)], axis=0)

    grad_in_ref[...] = lax.dot_general(rows(0), picks, TN, preferred_element_type=F32).astype(BF16)
    grad_out_ref[...] = lax.dot_general(rows(1), picks, TN, preferred_element_type=F32).T.astype(BF16)


def tokens_kernel(x_ref, cot_ref, send_ref):
    x = x_ref[...]
    total = cot_ref[3].astype(F32)
    combined = [None] * 4
    combined[3] = cot_ref[3]
    for b in (2, 1, 0):
        total = total + cot_ref[b].astype(F32)
        combined[b] = total.astype(BF16)
    first = 0
    for b, last in enumerate(LAST_OF_BAND):
        for k in range(first, last + 1):
            send_ref[k, 0] = x
            send_ref[k, 1] = combined[b]
        first = last + 1


def project(left_hidden, left_grad, weights_of, result_ref, target_ref, store_sem):
    part = result_ref.shape[-1]
    stores = []
    for z in range(Z):
        w_in, w_out = weights_of(z)
        for i, (left, right) in enumerate(((left_hidden, w_out), (left_grad, w_in))):
            whole = jnp.dot(left, right, preferred_element_type=F32).astype(BF16)
            for half in range(2):
                result_ref[2 * z + half, i] = whole[:, half * part : (half + 1) * part]
        blocks = pl.ds(2 * z, 2)
        store = pltpu.make_async_copy(result_ref.at[blocks], target_ref.at[blocks], store_sem.at[z])
        store.start()
        stores.append(store)
    return stores


def grads_kernel(
    own_ref, peer_ref, weights_ref, grads_ref, other_ref, hidden_ref, grad_pre_ref,
    x_ref, comb_ref, in_ref, out_ref, part_ref, theirs_ref, hid_ref, gpre_ref,
    token_sem, weight_sem, grad_sem, store_sem, keep_sem,
):
    count = own_ref.shape[1]
    width = weights_ref.shape[-1]
    full = in_ref.shape[-1]
    loads = ([], [])
    for i, (tokens, weights) in enumerate(((x_ref, in_ref), (comb_ref, out_ref))):
        for half, ref in enumerate((own_ref, peer_ref)):
            loads[i].append(
                pltpu.make_async_copy(
                    ref.at[i], tokens.at[pl.ds(half * count, count)], token_sem.at[2 * half + i]
                )
            )
        for z in range(Z):
            loads[i].append(
                pltpu.make_async_copy(
                    weights_ref.at[z, :, i], weights.at[:, :, pl.ds(z * width, width)], weight_sem.at[2 * z + i]
                )
            )
    for load in loads[0] + loads[1]:
        load.start()
    products = []
    for i, (tokens, weights) in enumerate(((x_ref, in_ref), (comb_ref, out_ref))):
        for load in loads[i]:
            load.wait()
        weight = weights[...].reshape(UNITS, full)
        products.append(lax.dot_general(tokens[...], weight, MXN, preferred_element_type=F32))
    pre, back = products
    square = pre * pre
    tangent = jnp.tanh(tanh_scale * (pre + cubic_term * square * pre))
    hid_ref[...] = (0.5 * pre * (1.0 + tangent)).astype(BF16)
    slope = 0.5 * (1.0 + tangent) + 0.5 * pre * (1.0 - tangent * tangent) * tanh_scale * (
        1.0 + 3.0 * cubic_term * square
    )
    gpre_ref[...] = (back * slope).astype(BF16)
    copies = [
        pltpu.make_async_copy(hid_ref.at[pl.ds(0, count)], hidden_ref, keep_sem.at[0]),
        pltpu.make_async_copy(gpre_ref.at[pl.ds(0, count)], grad_pre_ref, keep_sem.at[1]),
    ]
    for copy in copies:
        copy.start()

    def weights_of(z):
        lanes = slice(z * width, (z + 1) * width)
        return [ref[:, :, lanes].reshape(UNITS, width) for ref in (in_ref, out_ref)]

    copies += project(hid_ref[count:], gpre_ref[count:], weights_of, theirs_ref, other_ref, store_sem)
    turned = [left[...].T for left in (gpre_ref, hid_ref)]
    for z in range(Z):
        lanes = slice(z * width, (z + 1) * width)
        for i, tokens in enumerate((x_ref, comb_ref)):
            grad = jnp.dot(turned[i], tokens[:, lanes], preferred_element_type=F32)
            part_ref[z, :, i] = grad.astype(BF16).reshape(MP, HALF, width)
        copy = pltpu.make_async_copy(part_ref.at[z], grads_ref.at[z], grad_sem.at[z])
        copy.start()
        copies.append(copy)
    for copy in copies:
        copy.wait()


def own_kernel(
    hidden_ref, grad_pre_ref, weights_ref, own_ref,
    hid_ref, gpre_ref, held_ref, mine_ref, load_sem, weight_sem, store_sem,
):
    width = weights_ref.shape[-1]
    loads = [
        pltpu.make_async_copy(hidden_ref, hid_ref, load_sem.at[0]),
        pltpu.make_async_copy(grad_pre_ref, gpre_ref, load_sem.at[1]),
    ]
    pieces = [pltpu.make_async_copy(weights_ref.at[z], held_ref.at[z], weight_sem.at[z]) for z in range(Z)]
    for load in loads + pieces:
        load.start()
    for load in loads:
        load.wait()

    def weights_of(z):
        pieces[z].wait()
        return [held_ref[z, :, i].reshape(UNITS, width) for i in range(2)]

    for store in project(hid_ref[...], gpre_ref[...], weights_of, mine_ref, own_ref, store_sem):
        store.wait()


def sums_kernel(got_ref, outputs_ref, dx_ref):
    total = jnp.zeros(dx_ref.shape, F32)
    for k in range(MP):
        total = total + got_ref[k, 0].astype(F32)
        if k in LAST_OF_BAND:
            outputs_ref[LAST_OF_BAND.index(k)] = total.astype(BF16)
    total = jnp.zeros(dx_ref.shape, F32)
    for k in range(MP):
        total = total + got_ref[k, 1].astype(F32)
    dx_ref[...] = total.astype(BF16)


ANY = pl.BlockSpec(memory_space=pl.ANY)
VMEM = pl.BlockSpec(memory_space=pltpu.VMEM)
SMEM = pl.BlockSpec(memory_space=pltpu.SMEM)


def struct(*shape, dtype=BF16):
    return jax.ShapeDtypeStruct(shape, dtype)


def to_other_core(value):
    return lax.ppermute(value, "core", [(0, 1), (1, 0)])


def exchange(value):
    return lax.all_to_all(value, ("y", "x"), 0, 0, tiled=True)


def gate_kernel(*refs):
    del refs


def gate(value, earlier):
    return pl.pallas_call(
        gate_kernel,
        out_shape=struct(*value.shape),
        in_specs=[ANY, ANY],
        out_specs=ANY,
        input_output_aliases={0: 0},
        name="gate",
    )(value, earlier)


def per_device(features, w_in, w_out, unit_order, cotangents):
    core = lax.axis_index("core")
    count, part = features.shape
    units = unit_order.shape[0]
    width = 2 * part
    full = MP * part
    own, other, places = pl.pallas_call(
        sort_kernel,
        out_shape=(
            struct(MP, 2, HALF, part),
            struct(MP, 2, HALF, part),
            struct(1, units, dtype=jnp.int32),
        ),
        in_specs=[SMEM, VMEM, ANY, ANY],
        out_specs=(VMEM, VMEM, VMEM),
        scratch_shapes=[
            pltpu.VMEM(w_in.shape, BF16),
            pltpu.VMEM(w_out.shape, BF16),
            pltpu.SemaphoreType.DMA((2,)),
        ],
        compiler_params=params(),
        name="sort_units",
    )(core.reshape(1), unit_order.reshape(1, units), w_in, w_out)
    got = to_other_core(other)
    both = jnp.where(core == 0, jnp.concatenate([own, got], axis=3), jnp.concatenate([got, own], axis=3))
    mine = exchange(both)
    weights = lax.all_gather(mine.reshape(2 * UNITS, width), "z", axis=0, tiled=True)
    weights = weights.reshape(Z, MP, 2, HALF, width)

    send = pl.pallas_call(
        tokens_kernel,
        out_shape=struct(MP, 2, count, part),
        in_specs=[VMEM, VMEM],
        out_specs=VMEM,
        compiler_params=params(),
        name="combine_cotangents",
    )(features, cotangents)
    tokens = exchange(send)
    tokens = tokens.transpose(1, 2, 0, 3).reshape(2, count, full)
    peer_tokens = to_other_core(tokens)

    grads, out_other, hidden, grad_pre = pl.pallas_call(
        grads_kernel,
        out_shape=(
            struct(Z, MP, 2, HALF, width),
            struct(MP, 2, count, part),
            struct(count, UNITS),
            struct(count, UNITS),
        ),
        in_specs=[ANY] * 3,
        out_specs=(ANY,) * 4,
        scratch_shapes=[
            pltpu.VMEM((2 * count, full), BF16),
            pltpu.VMEM((2 * count, full), BF16),
            pltpu.VMEM((MP, HALF, full), BF16),
            pltpu.VMEM((MP, HALF, full), BF16),
            pltpu.VMEM((Z, MP, 2, HALF, width), BF16),
            pltpu.VMEM((MP, 2, count, part), BF16),
            pltpu.VMEM((2 * count, UNITS), BF16),
            pltpu.VMEM((2 * count, UNITS), BF16),
            pltpu.SemaphoreType.DMA((4,)),
            pltpu.SemaphoreType.DMA((2 * Z,)),
            pltpu.SemaphoreType.DMA((Z,)),
            pltpu.SemaphoreType.DMA((Z,)),
            pltpu.SemaphoreType.DMA((2,)),
        ],
        compiler_params=params(58),
        cost_estimate=pl.CostEstimate(
            flops=10 * UNITS * 2 * count * full, bytes_accessed=20 << 20, transcendentals=UNITS * 2 * count
        ),
        name="hidden_and_weight_grads",
    )(tokens, peer_tokens, weights)
    summed = lax.psum_scatter(grads.reshape(Z * 2 * UNITS, width), "z", scatter_dimension=0, tiled=True)
    summed = summed.reshape(MP, 2, HALF, width)

    out_own = pl.pallas_call(
        own_kernel,
        out_shape=struct(MP, 2, count, part),
        in_specs=[ANY] * 3,
        out_specs=ANY,
        scratch_shapes=[
            pltpu.VMEM((count, UNITS), BF16),
            pltpu.VMEM((count, UNITS), BF16),
            pltpu.VMEM((Z, MP, 2, HALF, width), BF16),
            pltpu.VMEM((MP, 2, count, part), BF16),
            pltpu.SemaphoreType.DMA((2,)),
            pltpu.SemaphoreType.DMA((Z,)),
            pltpu.SemaphoreType.DMA((Z,)),
        ],
        compiler_params=params(50),
        cost_estimate=pl.CostEstimate(flops=4 * UNITS * count * full, bytes_accessed=8 << 20, transcendentals=0),
        name="own_outputs_and_feature_grads",
    )(hidden, grad_pre, weights)
    out_peer = to_other_core(out_other)
    out_sum = (out_own.astype(F32) + out_peer.astype(F32)).astype(BF16)
    out_got = exchange(out_sum)
    rows = 128
    outputs, grad_features = pl.pallas_call(
        sums_kernel,
        grid=(count // rows,),
        out_shape=(struct(4, count, part), struct(count, part)),
        in_specs=[pl.BlockSpec((MP, 2, rows, part), lambda t: (0, 0, t, 0))],
        out_specs=(
            pl.BlockSpec((4, rows, part), lambda t: (0, t, 0)),
            pl.BlockSpec((rows, part), lambda t: (t, 0)),
        ),
        compiler_params=params(),
        name="sum_outputs",
    )(out_got)

    back = exchange(gate(summed, out_got))
    left, right = back[..., :part], back[..., part:]
    keep = jnp.where(core == 0, left, right)
    give = jnp.where(core == 0, right, left)
    grad_in, grad_out = pl.pallas_call(
        unsort_kernel,
        out_shape=(struct(part, units), struct(units, part)),
        in_specs=[VMEM, VMEM, VMEM],
        out_specs=(VMEM, VMEM),
        compiler_params=params(),
        name="unsort_grads",
    )(places, keep, to_other_core(give))
    return outputs, grad_features, grad_in, grad_out


def solution(mesh):
    whole = Mesh(mesh.devices.reshape(Z, 2, 4, 4), ("z", "core", "y", "x"))
    dp, mp = ("z", "core"), ("y", "x")
    return jax.shard_map(
        per_device,
        mesh=whole,
        in_specs=(P(dp, mp), P(dp, mp), P(mp, dp), P(mp), P(None, dp, mp)),
        out_specs=(P(None, dp, mp), P(dp, mp), P(dp, mp), P(mp, dp)),
        check_vma=False,
    )
```

time: 199 us -> 185 us (0.930)
  blocking collectives: 57.4 us -> 120 us
  waiting for transfers between devices: 70 us -> 11.9 us
  starting transfers between devices: 17.9 us -> 9.06 us
  local copies, waits for them, and re-layouts: 7.34 us -> 3.18 us
  other arithmetic: 4.91 us -> 1.4 us
    all_to_all x2 -> x4, blocking collectives: 57.4 us -> 120 us  [exchange(): return lax.all_to_all(value, ('y', 'x'), 0, 0, tiled=True)]
    reduce_scatter x1, waiting for transfers between devices: 28.4 us -> 0.84 us  [per_device(): lax.psum_scatter(grads.reshape(Z * 2 * UNITS, width), 'z', scatter_dimens...]
    all_to_all x2 -> x0, waiting for transfers between devices: 23.7 us -> none  [exchange(): return lax.all_to_all(value, ('y', 'x'), 0, 0, tiled=True)]
    all_to_all x2 -> x0, starting transfers between devices: 10.8 us -> none  [exchange(): return lax.all_to_all(value, ('y', 'x'), 0, 0, tiled=True)]
    ppermute x4, waiting for transfers between devices: 13.2 us -> 6.59 us  [to_other_core(): return lax.ppermute(value, 'core', [(0, 1), (1, 0)])]
    unnamed x18, local copies, waits for them, and re-layouts: 5.83 us -> 2.73 us
    pallas_call x1 -> x2, Pallas kernels: 8.91 us -> 6.05 us  [the longest x1 6.04 us: per_device(): pl.pallas_call(own_kernel, out_shape=struct(MP, 2, count, part), in_specs...]
  transfers between devices with their start and end apart: 8 -> 6, of which waited for: 8 -> 4; matrix products, arithmetic and copies ran while one was open for 3% -> 1% of each run, Pallas kernels for 6% -> 4%
where the time goes in v2:
time: 185 us
  blocking collectives  120 us (65%)
  Pallas kernels  25.3 us (14%)
  between operations  14.2 us (8%)
  waiting for transfers between devices  11.9 us (6%)
  starting transfers between devices  9.06 us (5%)
  local copies, waits for them, and re-layouts  3.18 us (2%)
    all_to_all x4, blocking collectives, exchange(): return lax.all_to_all(value, ('y', 'x'), 0, 0, tiled=True)  120 us
    pallas_call x1, Pallas kernels, per_device(): pl.pallas_call(grads_kernel, out_shape=(struct(Z, MP, 2, HALF, width), st...  13 us
    ppermute x4, starting transfers between devices, to_other_core(): return lax.ppermute(value, 'core', [(0, 1), (1, 0)])  8.99 us
    ppermute x4, waiting for transfers between devices, to_other_core(): return lax.ppermute(value, 'core', [(0, 1), (1, 0)])  6.59 us
    pallas_call x1, Pallas kernels, per_device(): pl.pallas_call(own_kernel, out_shape=struct(MP, 2, count, part), in_specs...  6.04 us
    all_gather x1, waiting for transfers between devices, per_device(): lax.all_gather(mine.reshape(2 * UNITS, width), 'z', axis=0, tiled=True)  4.42 us
  transfers between devices with their start and end apart: 6, of which 4 were waited for; matrix products, arithmetic and copies ran while one was open for 1% of the time, Pallas kernels for 4%

profile of v2, /device:TPU:1, one launch (start us, length us, event | category | flops | bytes accessed | tf_op | source)
XLA Modules:
  0.0 184.6 jit_solution(2242926435980997284)
XLA Ops:
  7.2 1.0 copy-done.4
  8.2 0.9 copy-done.5
  9.2 0.7 copy-done.7
  9.9 2.1 %sort_units.1 = (bf16[16,2,32,128]{3,2,1,0:T(8,128)(2,1)S(1)}, bf16[16,2,32,128]{3,2,1,0:T(8,128)(2,1)S(1)}, s32[1,1024]{1,0:T(1,128)S(1)}) custom-call(s32[1]{0:T(128)} %bitcast.1.core_ref, s32[1,1024]{1,0:T(1,128)S(1)} %bitcast.12, bf16[128,1024]{1,0:T(8,128)(2,1)S(1)} %copy-done.4, bf16[1024,128]{1,0:T(8,128)(2,1)S(1)} %copy-done.5), custom_call_target="tpu_custom_call" | custom-call | tf_op jit(solution)/shard_map/sort_units/pallas_call | solution.py:257
  12.0 3.3 %collective-permute-start.1 = (bf16[16,2,32,128]{3,2,1,0:T(8,128)(2,1)S(1)}, bf16[16,2,32,128]{3,2,1,0:T(8,128)(2,1)S(1)}, u32[]{:S(2)}, u32[]{:S(2)}) collective-permute-start(bf16[16,2,32,128]{3,2,1,0:T(8,128)(2,1)S(1)} %get-tuple-element.16), channel_id=1, source_target_pairs={{0,16},{16,0},{1,17},{17,1},{2,18},{18,2},{3,19},{19,3},{4,20},{20... | collective-permute-start | bytes 786440 | tf_op jit(solution)/shard_map/ppermute | solution.py:229
  15.3 1.2 collective-permute-done.1
  16.5 0.3 maximum_select_fusion
  16.8 15.6 %all_to_all.20 = bf16[16,2,32,256]{3,2,1,0:T(8,128)(2,1)} all-to-all(bf16[16,2,32,256]{3,2,1,0:T(8,128)(2,1)S(1)} %maximum_select_fusion), channel_id=1, replica_groups=mesh['z'=8,'core'=2,'y'=4,'x'=4] {'y','x'}, dimensions={0} | all-to-all | bytes 1048576 | tf_op jit(solution)/shard_map/all_to_all | solution.py:233
  32.5 0.5 combine_cotangents.1
  33.0 41.8 %all_to_all.21 = bf16[16,2,384,128]{3,2,1,0:T(8,128)(2,1)S(1)} all-to-all(bf16[16,2,384,128]{3,2,1,0:T(8,128)(2,1)S(1)} %combine_cotangents.1), channel_id=1, replica_groups=mesh['z'=8,'core'=2,'y'=4,'x'=4] {'y','x'}, dimensions={0} | all-to-all | bytes 6291456 | tf_op jit(solution)/shard_map/all_to_all | solution.py:233
  74.7 0.4 copy_bitcast_fusion.own_ref
  75.2 2.5 %collective-permute-start = (bf16[2,384,2048]{2,1,0:T(8,128)(2,1)S(1)}, bf16[2,384,2048]{2,1,0:T(8,128)(2,1)}, u32[]{:S(2)}, u32[]{:S(2)}) collective-permute-start(bf16[2,384,2048]{2,1,0:T(8,128)(2,1)S(1)} %copy_bitcast_fusion.own_ref), channel_id=1, source_target_pairs={{0,16},{16,0},{1,17},{17,1},{2,18},{18,2},{3,19},{19,3},{4,20},{20... | collective-permute-start | bytes 9437192 | tf_op jit(solution)/shard_map/ppermute | solution.py:229
  77.7 5.4 %collective-permute-done.peer_ref = bf16[2,384,2048]{2,1,0:T(8,128)(2,1)} collective-permute-done((bf16[2,384,2048]{2,1,0:T(8,128)(2,1)S(1)}, bf16[2,384,2048]{2,1,0:T(8,128)(2,1)}, u32[]{:S(2)}, u32[]{:S(2)}) %collective-permute-start) | collective-permute-done | bytes 3145760 | tf_op jit(solution)/shard_map/ppermute | solution.py:229
  83.2 4.4 %all-gather.2.cloned.1.call-done = bf16[8192,256]{1,0:T(8,128)(2,1)} async-done(((bf16[1024,256]{1,0:T(8,128)(2,1)}), bf16[8192,256]{1,0:T(8,128)(2,1)}) %all-gather.2.cloned.1.call-update) | async-done | bytes 4194320 | tf_op jit(solution)/shard_map/all_gather | solution.py:277
  87.6 13.0 %hidden_and_weight_grads.1 = (bf16[8,16,2,32,256]{4,3,2,1,0:T(8,128)(2,1)}, bf16[16,2,384,128]{3,2,1,0:T(8,128)(2,1)}, bf16[384,512]{1,0:T(8,128)(2,1)}, bf16[384,512]{1,0:T(8,128)(2,1)}) custom-call(bf16[2,384,2048]{2,1,0:T(8,128)(2,1)} %copy-done.8, bf16[2,384,2048]{2,1,0:T(8,128)(2,1)} %collective-permute-done.peer_ref, bf16[8,16,2,32,256]{4,3,2,1,0:T(8,128)(2,1)} %bitcast.13), custom_call_target="tpu_custom_call" | custom-call | flops 8053063680 | bytes 20971520 | tf_op jit(solution)/shard_map/hidden_and_weight_grads/pallas_call | solution.py:292
  100.7 1.0 collective-permute-start.2
  101.8 6.0 %own_outputs_and_feature_grads.1 = bf16[16,2,384,128]{3,2,1,0:T(8,128)(2,1)S(1)} custom-call(bf16[384,512]{1,0:T(8,128)(2,1)S(1)} %copy-done.1, bf16[384,512]{1,0:T(8,128)(2,1)S(1)} %copy-done.2, bf16[8,16,2,32,256]{4,3,2,1,0:T(8,128)(2,1)} %bitcast.14), custom_call_target="tpu_custom_call" | custom-call | flops 1610612736 | bytes 8388608 | tf_op jit(solution)/shard_map/own_outputs_and_feature_grads/pallas_call | solution.py:326
  107.8 1.1 add_convert_fusion
  108.9 45.0 %all_to_all.22.got_ref.refs_1_ = bf16[16,2,384,128]{3,2,1,0:T(8,128)(2,1)} all-to-all(bf16[16,2,384,128]{3,2,1,0:T(8,128)(2,1)S(1)} %add_convert_fusion), channel_id=1, replica_groups=mesh['z'=8,'core'=2,'y'=4,'x'=4] {'y','x'}, dimensions={0} | all-to-all | bytes 6291456 | tf_op jit(solution)/shard_map/all_to_all | solution.py:233
  154.0 0.8 reduce-scatter.2.cloned.1.call-done
  154.8 17.2 %all_to_all.23 = bf16[16,2,32,256]{3,2,1,0:T(8,128)(2,1)S(1)} all-to-all(bf16[16,2,32,256]{3,2,1,0:T(8,128)(2,1)} %gate.1), channel_id=1, replica_groups=mesh['z'=8,'core'=2,'y'=4,'x'=4] {'y','x'}, dimensions={0} | all-to-all | bytes 1048576 | tf_op jit(solution)/shard_map/all_to_all | solution.py:233
  172.1 2.1 %collective-permute-start.3 = (bf16[16,2,32,128]{3,2,1,0:T(8,128)(2,1)S(1)}, bf16[16,2,32,128]{3,2,1,0:T(8,128)(2,1)S(1)}, u32[]{:S(2)}, u32[]{:S(2)}) collective-permute-start(bf16[16,2,32,128]{3,2,1,0:T(8,128)(2,1)S(1)} %get-tuple-element.26), channel_id=1, source_target_pairs={{0,16},{16,0},{1,17},{17,1},{2,18},{18,2},{3,19},{19,3},{4,20},{20... | collective-permute-start | bytes 786440 | tf_op jit(solution)/shard_map/ppermute | solution.py:229
  174.2 1.8 sum_outputs.1
  176.0 1.8 unsort_grads.1
  (23 shorter events, 0.3 us)
Async XLA Ops:
  7.2 25.3 %copy-start.3 = (bf16[4,384,128]{2,1,0:T(8,128)(2,1)S(1)}, bf16[4,384,128]{2,1,0:T(8,128)(2,1)}, u32[]{:S(2)}) copy-start(bf16[4,384,128]{2,1,0:T(8,128)(2,1)} %cot_ref.1) | copy-start | bytes 1179652
  7.2 80.4 %all-gather.2.cloned.1.call-start = ((), (), s32[]{:S(2)}) async-start(), calls=%async_computation.5 | async-start | bytes 4718592 | tf_op jit(solution)/shard_map/all_gather | solution.py:277
  7.2 1.0 copy-start.4
  8.2 0.9 copy-start.5
  9.2 0.7 copy-start.7
  9.9 22.6 %copy-start.6 = (bf16[384,128]{1,0:T(8,128)(2,1)S(1)}, bf16[384,128]{1,0:T(8,128)(2,1)}, u32[]{:S(2)}) copy-start(bf16[384,128]{1,0:T(8,128)(2,1)} %x_ref.1) | copy-start | bytes 294916
  12.0 4.5 %collective-permute-start.1 = (bf16[16,2,32,128]{3,2,1,0:T(8,128)(2,1)S(1)}, bf16[16,2,32,128]{3,2,1,0:T(8,128)(2,1)S(1)}, u32[]{:S(2)}, u32[]{:S(2)}) collective-permute-start(bf16[16,2,32,128]{3,2,1,0:T(8,128)(2,1)S(1)} %get-tuple-element.16), channel_id=1, source_target_pairs={{0,16},{16,0},{1,17},{17,1},{2,18},{18,2},{3,19},{19,3},{4,20},{20... | collective-permute-start | bytes 786440 | tf_op jit(solution)/shard_map/ppermute | solution.py:229
  32.4 122.4 %reduce-scatter.2.cloned.1.call-start = ((), (), s32[]{:S(2)}) async-start(), calls=%async_computation.6 | async-start | bytes 4718592 | tf_op jit(solution)/shard_map/reduce_scatter | solution.py:323
  75.2 12.4 %copy-start.8 = (bf16[2,384,2048]{2,1,0:T(8,128)(2,1)}, bf16[2,384,2048]{2,1,0:T(8,128)(2,1)S(1)}, u32[]{:S(2)}) copy-start(bf16[2,384,2048]{2,1,0:T(8,128)(2,1)S(1)} %copy_bitcast_fusion.own_ref) | copy-start | bytes 9437188
  75.2 8.0 %collective-permute-start = (bf16[2,384,2048]{2,1,0:T(8,128)(2,1)S(1)}, bf16[2,384,2048]{2,1,0:T(8,128)(2,1)}, u32[]{:S(2)}, u32[]{:S(2)}) collective-permute-start(bf16[2,384,2048]{2,1,0:T(8,128)(2,1)S(1)} %copy_bitcast_fusion.own_ref), channel_id=1, source_target_pairs={{0,16},{16,0},{1,17},{17,1},{2,18},{18,2},{3,19},{19,3},{4,20},{20... | collective-permute-start | bytes 9437192 | tf_op jit(solution)/shard_map/ppermute | solution.py:229
  100.6 1.0 copy-start.1
  100.6 1.1 copy-start.2
  100.7 7.1 %collective-permute-start.2 = (bf16[16,2,384,128]{3,2,1,0:T(8,128)(2,1)}, bf16[16,2,384,128]{3,2,1,0:T(8,128)(2,1)S(1)}, u32[]{:S(2)}, u32[]{:S(2)}) collective-permute-start(bf16[16,2,384,128]{3,2,1,0:T(8,128)(2,1)} %get-tuple-element.19), channel_id=1, source_target_pairs={{0,16},{16,0},{1,17},{17,1},{2,18},{18,2},{3,19},{19,3},{4,20},{20... | collective-permute-start | bytes 9437192 | tf_op jit(solution)/shard_map/ppermute | solution.py:229
  154.8 19.4 %copy-start = (bf16[16,2,384,128]{3,2,1,0:T(8,128)(2,1)S(1)}, bf16[16,2,384,128]{3,2,1,0:T(8,128)(2,1)}, u32[]{:S(2)}) copy-start(bf16[16,2,384,128]{3,2,1,0:T(8,128)(2,1)} %all_to_all.22.got_ref.refs_1_) | copy-start | bytes 9437188
  172.1 3.9 %collective-permute-start.3 = (bf16[16,2,32,128]{3,2,1,0:T(8,128)(2,1)S(1)}, bf16[16,2,32,128]{3,2,1,0:T(8,128)(2,1)S(1)}, u32[]{:S(2)}, u32[]{:S(2)}) collective-permute-start(bf16[16,2,32,128]{3,2,1,0:T(8,128)(2,1)S(1)} %get-tuple-element.26), channel_id=1, source_target_pairs={{0,16},{16,0},{1,17},{17,1},{2,18},{18,2},{3,19},{19,3},{4,20},{20... | collective-permute-start | bytes 786440 | tf_op jit(solution)/shard_map/ppermute | solution.py:229
Sparse Core Ops, SparseCore 0:
  32.5 54.9 all-gather.1
  100.8 53.9 reduce-scatter.1

commit v3 on v2

--- a/solution.py
+++ b/solution.py
@@ -34,14 +34,17 @@
 
 
 def sort_kernel(
-    core_ref, units_ref, w_in_hbm, w_out_hbm, own_ref, other_ref, places_ref, w_in_ref, w_out_ref, load_sem
+    core_ref, units_hbm, w_in_hbm, w_out_hbm, own_ref, other_ref, places_ref,
+    units_ref, w_in_ref, w_out_ref, load_sem,
 ):
-    loads = [
-        pltpu.make_async_copy(w_in_hbm, w_in_ref, load_sem.at[0]),
-        pltpu.make_async_copy(w_out_hbm, w_out_ref, load_sem.at[1]),
+    first, *loads = [
+        pltpu.make_async_copy(units_hbm, units_ref, load_sem.at[0]),
+        pltpu.make_async_copy(w_in_hbm, w_in_ref, load_sem.at[1]),
+        pltpu.make_async_copy(w_out_hbm, w_out_ref, load_sem.at[2]),
     ]
-    for load in loads:
+    for load in (first, *loads):
         load.start()
+    first.wait()
     units = units_ref[...]
     size = units.shape[1]
     band = (
@@ -225,6 +228,10 @@
     return jax.ShapeDtypeStruct(shape, dtype)
 
 
+def in_hbm(value):
+    return pltpu.with_memory_space_constraint(value, pltpu.HBM)
+
+
 def to_other_core(value):
     return lax.ppermute(value, "core", [(0, 1), (1, 0)])
 
@@ -245,7 +252,7 @@
         out_specs=ANY,
         input_output_aliases={0: 0},
         name="gate",
-    )(value, earlier)
+    )(in_hbm(value), earlier)
 
 
 def per_device(features, w_in, w_out, unit_order, cotangents):
@@ -261,16 +268,17 @@
             struct(MP, 2, HALF, part),
             struct(1, units, dtype=jnp.int32),
         ),
-        in_specs=[SMEM, VMEM, ANY, ANY],
+        in_specs=[SMEM, ANY, ANY, ANY],
         out_specs=(VMEM, VMEM, VMEM),
         scratch_shapes=[
+            pltpu.VMEM((1, units), jnp.int32),
             pltpu.VMEM(w_in.shape, BF16),
             pltpu.VMEM(w_out.shape, BF16),
-            pltpu.SemaphoreType.DMA((2,)),
+            pltpu.SemaphoreType.DMA((3,)),
         ],
         compiler_params=params(),
         name="sort_units",
-    )(core.reshape(1), unit_order.reshape(1, units), w_in, w_out)
+    )(core.reshape(1), *map(in_hbm, (unit_order.reshape(1, units), w_in, w_out)))
     got = to_other_core(other)
     both = jnp.where(core == 0, jnp.concatenate([own, got], axis=3), jnp.concatenate([got, own], axis=3))
     mine = exchange(both)
@@ -340,7 +348,7 @@
         compiler_params=params(50),
         cost_estimate=pl.CostEstimate(flops=4 * UNITS * count * full, bytes_accessed=8 << 20, transcendentals=0),
         name="own_outputs_and_feature_grads",
-    )(hidden, grad_pre, weights)
+    )(*map(in_hbm, (hidden, grad_pre, weights)))
     out_peer = to_other_core(out_other)
     out_sum = (out_own.astype(F32) + out_peer.astype(F32)).astype(BF16)
     out_got = exchange(out_sum)

time: 185 us -> 183 us (0.989)
  blocking collectives: 120 us -> 118 us
  transfers between devices with their start and end apart: 6 -> 6, of which waited for: 4 -> 3; matrix products, arithmetic and copies ran while one was open for 1% -> 1% of each run, Pallas kernels for 4% -> 5%
where the time goes in v3:
time: 183 us
  blocking collectives  118 us (64%)
  Pallas kernels  26.9 us (15%)
  between operations  14.2 us (8%)
  waiting for transfers between devices  11.1 us (6%)
  starting transfers between devices  8.75 us (5%)
  local copies, waits for them, and re-layouts  2.32 us (1%)
    all_to_all x4, blocking collectives, exchange(): return lax.all_to_all(value, ('y', 'x'), 0, 0, tiled=True)  118 us
    pallas_call x1, Pallas kernels, per_device(): pl.pallas_call(grads_kernel, out_shape=(struct(Z, MP, 2, HALF, width), st...  13 us
    ppermute x4, starting transfers between devices, to_other_core(): return lax.ppermute(value, 'core', [(0, 1), (1, 0)])  8.67 us
    pallas_call x1, Pallas kernels, per_device(): pl.pallas_call(own_kernel, out_shape=struct(MP, 2, count, part), in_specs...  6.9 us
    ppermute x4, waiting for transfers between devices, to_other_core(): return lax.ppermute(value, 'core', [(0, 1), (1, 0)])  6.59 us
    all_gather x1, waiting for transfers between devices, per_device(): lax.all_gather(mine.reshape(2 * UNITS, width), 'z', axis=0, tiled=True)  4.43 us
  transfers between devices with their start and end apart: 6, of which 3 were waited for; matrix products, arithmetic and copies ran while one was open for 1% of the time, Pallas kernels for 5%

profile of v3, /device:TPU:1, one launch (start us, length us, event | category | flops | bytes accessed | tf_op | source)
XLA Modules:
  0.0 182.7 jit_solution(4534610141010785044)
XLA Ops:
  7.2 0.0 all-gather.2.cloned.1.call-start
  7.2 2.8 %sort_units.1 = (bf16[16,2,32,128]{3,2,1,0:T(8,128)(2,1)S(1)}, bf16[16,2,32,128]{3,2,1,0:T(8,128)(2,1)S(1)}, s32[1,1024]{1,0:T(1,128)S(1)}) custom-call(s32[1]{0:T(128)} %bitcast.1.core_ref, s32[1,1024]{1,0:T(1,128)} %bitcast.17, bf16[128,1024]{1,0:T(8,128)(2,1)} %w_in_hbm.1, bf16[1024,128]{1,0:T(8,128)(2,1)} %w_out_hbm.1), custom_call_target="tpu_custom_call" | custom-call | tf_op jit(solution)/shard_map/sort_units/pallas_call | solution.py:264
  10.1 3.3 %collective-permute-start.1 = (bf16[16,2,32,128]{3,2,1,0:T(8,128)(2,1)S(1)}, bf16[16,2,32,128]{3,2,1,0:T(8,128)(2,1)S(1)}, u32[]{:S(2)}, u32[]{:S(2)}) collective-permute-start(bf16[16,2,32,128]{3,2,1,0:T(8,128)(2,1)S(1)} %get-tuple-element.16), channel_id=1, source_target_pairs={{0,16},{16,0},{1,17},{17,1},{2,18},{18,2},{3,19},{19,3},{4,20},{20... | collective-permute-start | bytes 786440 | tf_op jit(solution)/shard_map/ppermute | solution.py:236
  13.4 1.2 collective-permute-done.1
  14.6 0.3 maximum_select_fusion
  14.8 15.6 %all_to_all.20 = bf16[16,2,32,256]{3,2,1,0:T(8,128)(2,1)} all-to-all(bf16[16,2,32,256]{3,2,1,0:T(8,128)(2,1)S(1)} %maximum_select_fusion), channel_id=1, replica_groups=mesh['z'=8,'core'=2,'y'=4,'x'=4] {'y','x'}, dimensions={0} | all-to-all | bytes 1048576 | tf_op jit(solution)/shard_map/all_to_all | solution.py:240
  30.5 0.0 all-gather.2.cloned.1.call-update
  30.5 0.0 reduce-scatter.2.cloned.1.call-start
  30.6 0.5 combine_cotangents.1
  31.1 41.8 %all_to_all.21 = bf16[16,2,384,128]{3,2,1,0:T(8,128)(2,1)S(1)} all-to-all(bf16[16,2,384,128]{3,2,1,0:T(8,128)(2,1)S(1)} %combine_cotangents.1), channel_id=1, replica_groups=mesh['z'=8,'core'=2,'y'=4,'x'=4] {'y','x'}, dimensions={0} | all-to-all | bytes 6291456 | tf_op jit(solution)/shard_map/all_to_all | solution.py:240
  72.8 0.4 copy_bitcast_fusion.own_ref
  73.3 2.5 %collective-permute-start = (bf16[2,384,2048]{2,1,0:T(8,128)(2,1)S(1)}, bf16[2,384,2048]{2,1,0:T(8,128)(2,1)}, u32[]{:S(2)}, u32[]{:S(2)}) collective-permute-start(bf16[2,384,2048]{2,1,0:T(8,128)(2,1)S(1)} %copy_bitcast_fusion.own_ref), channel_id=1, source_target_pairs={{0,16},{16,0},{1,17},{17,1},{2,18},{18,2},{3,19},{19,3},{4,20},{20... | collective-permute-start | bytes 9437192 | tf_op jit(solution)/shard_map/ppermute | solution.py:236
  75.8 5.4 %collective-permute-done.peer_ref = bf16[2,384,2048]{2,1,0:T(8,128)(2,1)} collective-permute-done((bf16[2,384,2048]{2,1,0:T(8,128)(2,1)S(1)}, bf16[2,384,2048]{2,1,0:T(8,128)(2,1)}, u32[]{:S(2)}, u32[]{:S(2)}) %collective-permute-start) | collective-permute-done | bytes 3145760 | tf_op jit(solution)/shard_map/ppermute | solution.py:236
  81.2 4.4 %all-gather.2.cloned.1.call-done = bf16[8192,256]{1,0:T(8,128)(2,1)} async-done(((bf16[1024,256]{1,0:T(8,128)(2,1)}), bf16[8192,256]{1,0:T(8,128)(2,1)}) %all-gather.2.cloned.1.call-update) | async-done | bytes 4194320 | tf_op jit(solution)/shard_map/all_gather | solution.py:285
  85.7 13.0 %hidden_and_weight_grads.1 = (bf16[8,16,2,32,256]{4,3,2,1,0:T(8,128)(2,1)}, bf16[16,2,384,128]{3,2,1,0:T(8,128)(2,1)}, bf16[384,512]{1,0:T(8,128)(2,1)}, bf16[384,512]{1,0:T(8,128)(2,1)}) custom-call(bf16[2,384,2048]{2,1,0:T(8,128)(2,1)} %copy-done.3, bf16[2,384,2048]{2,1,0:T(8,128)(2,1)} %collective-permute-done.peer_ref, bf16[8,16,2,32,256]{4,3,2,1,0:T(8,128)(2,1)} %bitcast.12), custom_call_target="tpu_custom_call" | custom-call | flops 8053063680 | bytes 20971520 | tf_op jit(solution)/shard_map/hidden_and_weight_grads/pallas_call | solution.py:300
  98.8 1.9 %copy-done.4 = bf16[16,2,384,128]{3,2,1,0:T(8,128)(2,1)S(1)} copy-done((bf16[16,2,384,128]{3,2,1,0:T(8,128)(2,1)S(1)}, bf16[16,2,384,128]{3,2,1,0:T(8,128)(2,1)}, u32[]{:S(2)}) %copy-start.4) | copy-done | bytes 3145752
  100.6 0.7 collective-permute-start.2
  101.3 6.9 %own_outputs_and_feature_grads.1 = bf16[16,2,384,128]{3,2,1,0:T(8,128)(2,1)S(1)} custom-call(bf16[384,512]{1,0:T(8,128)(2,1)} %get-tuple-element.17.hidden_ref, bf16[384,512]{1,0:T(8,128)(2,1)} %get-tuple-element.18.grad_pre_ref, bf16[8,16,2,32,256]{4,3,2,1,0:T(8,128)(2,1)} %bitcast.13), custom_call_target="tpu_custom_call" | custom-call | flops 1610612736 | bytes 8388608 | tf_op jit(solution)/shard_map/own_outputs_and_feature_grads/pallas_call | solution.py:334
  108.2 1.1 add_convert_fusion
  109.3 45.8 %all_to_all.22.got_ref.refs_1_ = bf16[16,2,384,128]{3,2,1,0:T(8,128)(2,1)} all-to-all(bf16[16,2,384,128]{3,2,1,0:T(8,128)(2,1)S(1)} %add_convert_fusion), channel_id=1, replica_groups=mesh['z'=8,'core'=2,'y'=4,'x'=4] {'y','x'}, dimensions={0} | all-to-all | bytes 6291456 | tf_op jit(solution)/shard_map/all_to_all | solution.py:240
  155.2 14.9 %all_to_all.23 = bf16[16,2,32,256]{3,2,1,0:T(8,128)(2,1)S(1)} all-to-all(bf16[16,2,32,256]{3,2,1,0:T(8,128)(2,1)} %gate.1), channel_id=1, replica_groups=mesh['z'=8,'core'=2,'y'=4,'x'=4] {'y','x'}, dimensions={0} | all-to-all | bytes 1048576 | tf_op jit(solution)/shard_map/all_to_all | solution.py:240
  170.1 2.1 %collective-permute-start.3 = (bf16[16,2,32,128]{3,2,1,0:T(8,128)(2,1)S(1)}, bf16[16,2,32,128]{3,2,1,0:T(8,128)(2,1)S(1)}, u32[]{:S(2)}, u32[]{:S(2)}) collective-permute-start(bf16[16,2,32,128]{3,2,1,0:T(8,128)(2,1)S(1)} %get-tuple-element.26), channel_id=1, source_target_pairs={{0,16},{16,0},{1,17},{17,1},{2,18},{18,2},{3,19},{19,3},{4,20},{20... | collective-permute-start | bytes 786440 | tf_op jit(solution)/shard_map/ppermute | solution.py:236
  172.3 1.8 sum_outputs.1
  174.1 1.8 %unsort_grads.1 = (bf16[128,1024]{1,0:T(8,128)(2,1)}, bf16[1024,128]{1,0:T(8,128)(2,1)}) custom-call(s32[1,1024]{1,0:T(1,128)S(1)} %get-tuple-element.22.places_ref, bf16[16,2,32,128]{3,2,1,0:T(8,128)(2,1)S(1)} %get-tuple-element.27.own_ref, bf16[16,2,32,128]{3,2,1,0:T(8,128)(2,1)S(1)} %collective-permute-done.3.other_ref), custom_call_target="tpu_custom_call" | custom-call | tf_op jit(solution)/shard_map/unsort_grads/pallas_call | solution.py:373
  (15 shorter events, 0.1 us)
Async XLA Ops:
  7.2 23.4 %copy-start.1 = (bf16[4,384,128]{2,1,0:T(8,128)(2,1)S(1)}, bf16[4,384,128]{2,1,0:T(8,128)(2,1)}, u32[]{:S(2)}) copy-start(bf16[4,384,128]{2,1,0:T(8,128)(2,1)} %cot_ref.1) | copy-start | bytes 1179652
  7.2 23.4 %copy-start.2 = (bf16[384,128]{1,0:T(8,128)(2,1)S(1)}, bf16[384,128]{1,0:T(8,128)(2,1)}, u32[]{:S(2)}) copy-start(bf16[384,128]{1,0:T(8,128)(2,1)} %x_ref.1) | copy-start | bytes 294916
  7.2 78.5 %all-gather.2.cloned.1.call-start = ((), (), s32[]{:S(2)}) async-start(), calls=%async_computation.5 | async-start | bytes 4718592 | tf_op jit(solution)/shard_map/all_gather | solution.py:285
  10.1 4.5 %collective-permute-start.1 = (bf16[16,2,32,128]{3,2,1,0:T(8,128)(2,1)S(1)}, bf16[16,2,32,128]{3,2,1,0:T(8,128)(2,1)S(1)}, u32[]{:S(2)}, u32[]{:S(2)}) collective-permute-start(bf16[16,2,32,128]{3,2,1,0:T(8,128)(2,1)S(1)} %get-tuple-element.16), channel_id=1, source_target_pairs={{0,16},{16,0},{1,17},{17,1},{2,18},{18,2},{3,19},{19,3},{4,20},{20... | collective-permute-start | bytes 786440 | tf_op jit(solution)/shard_map/ppermute | solution.py:236
  30.5 124.7 %reduce-scatter.2.cloned.1.call-start = ((), (), s32[]{:S(2)}) async-start(), calls=%async_computation.6 | async-start | bytes 4718592 | tf_op jit(solution)/shard_map/reduce_scatter | solution.py:331
  73.3 12.4 %copy-start.3 = (bf16[2,384,2048]{2,1,0:T(8,128)(2,1)}, bf16[2,384,2048]{2,1,0:T(8,128)(2,1)S(1)}, u32[]{:S(2)}) copy-start(bf16[2,384,2048]{2,1,0:T(8,128)(2,1)S(1)} %copy_bitcast_fusion.own_ref) | copy-start | bytes 9437188
  73.3 8.0 %collective-permute-start = (bf16[2,384,2048]{2,1,0:T(8,128)(2,1)S(1)}, bf16[2,384,2048]{2,1,0:T(8,128)(2,1)}, u32[]{:S(2)}, u32[]{:S(2)}) collective-permute-start(bf16[2,384,2048]{2,1,0:T(8,128)(2,1)S(1)} %copy_bitcast_fusion.own_ref), channel_id=1, source_target_pairs={{0,16},{16,0},{1,17},{17,1},{2,18},{18,2},{3,19},{19,3},{4,20},{20... | collective-permute-start | bytes 9437192 | tf_op jit(solution)/shard_map/ppermute | solution.py:236
  98.7 1.9 %copy-start.4 = (bf16[16,2,384,128]{3,2,1,0:T(8,128)(2,1)S(1)}, bf16[16,2,384,128]{3,2,1,0:T(8,128)(2,1)}, u32[]{:S(2)}) copy-start(bf16[16,2,384,128]{3,2,1,0:T(8,128)(2,1)} %get-tuple-element.19) | copy-start | bytes 9437188
  100.6 7.6 %collective-permute-start.2 = (bf16[16,2,384,128]{3,2,1,0:T(8,128)(2,1)S(1)}, bf16[16,2,384,128]{3,2,1,0:T(8,128)(2,1)S(1)}, u32[]{:S(2)}, u32[]{:S(2)}) collective-permute-start(bf16[16,2,384,128]{3,2,1,0:T(8,128)(2,1)S(1)} %copy-done.4), channel_id=1, source_target_pairs={{0,16},{16,0},{1,17},{17,1},{2,18},{18,2},{3,19},{19,3},{4,20},{20... | collective-permute-start | bytes 9437192 | tf_op jit(solution)/shard_map/ppermute | solution.py:236
  155.2 17.1 %copy-start = (bf16[16,2,384,128]{3,2,1,0:T(8,128)(2,1)S(1)}, bf16[16,2,384,128]{3,2,1,0:T(8,128)(2,1)}, u32[]{:S(2)}) copy-start(bf16[16,2,384,128]{3,2,1,0:T(8,128)(2,1)} %all_to_all.22.got_ref.refs_1_) | copy-start | bytes 9437188
  170.1 3.9 %collective-permute-start.3 = (bf16[16,2,32,128]{3,2,1,0:T(8,128)(2,1)S(1)}, bf16[16,2,32,128]{3,2,1,0:T(8,128)(2,1)S(1)}, u32[]{:S(2)}, u32[]{:S(2)}) collective-permute-start(bf16[16,2,32,128]{3,2,1,0:T(8,128)(2,1)S(1)} %get-tuple-element.26), channel_id=1, source_target_pairs={{0,16},{16,0},{1,17},{17,1},{2,18},{18,2},{3,19},{19,3},{4,20},{20... | collective-permute-start | bytes 786440 | tf_op jit(solution)/shard_map/ppermute | solution.py:236
Sparse Core Ops, SparseCore 0:
  30.6 54.9 all-gather.1
  98.9 53.9 reduce-scatter.1

commit v4 on v3

--- a/solution.py
+++ b/solution.py
@@ -348,7 +348,7 @@
         compiler_params=params(50),
         cost_estimate=pl.CostEstimate(flops=4 * UNITS * count * full, bytes_accessed=8 << 20, transcendentals=0),
         name="own_outputs_and_feature_grads",
-    )(*map(in_hbm, (hidden, grad_pre, weights)))
+    )(hidden, grad_pre, weights)
     out_peer = to_other_core(out_other)
     out_sum = (out_own.astype(F32) + out_peer.astype(F32)).astype(BF16)
     out_got = exchange(out_sum)

time: 183 us -> 183 us (level)
  blocking collectives: 118 us -> 120 us
  transfers between devices with their start and end apart: 6 -> 6, of which waited for: 3 -> 4; matrix products, arithmetic and copies ran while one was open for 1% -> 1% of each run, Pallas kernels for 5% -> 5%
where the time goes in v4:
time: 183 us
  blocking collectives  120 us (66%)
  Pallas kernels  26 us (14%)
  between operations  14.2 us (8%)
  waiting for transfers between devices  11.9 us (7%)
  starting transfers between devices  9.05 us (5%)
    all_to_all x4, blocking collectives, exchange(): return lax.all_to_all(value, ('y', 'x'), 0, 0, tiled=True)  120 us
    pallas_call x1, Pallas kernels, per_device(): pl.pallas_call(grads_kernel, out_shape=(struct(Z, MP, 2, HALF, width), st...  13 us
    ppermute x4, starting transfers between devices, to_other_core(): return lax.ppermute(value, 'core', [(0, 1), (1, 0)])  8.98 us
    ppermute x4, waiting for transfers between devices, to_other_core(): return lax.ppermute(value, 'core', [(0, 1), (1, 0)])  6.59 us
    pallas_call x1, Pallas kernels, per_device(): pl.pallas_call(own_kernel, out_shape=struct(MP, 2, count, part), in_specs...  6.04 us
    all_gather x1, waiting for transfers between devices, per_device(): lax.all_gather(mine.reshape(2 * UNITS, width), 'z', axis=0, tiled=True)  4.43 us
  transfers between devices with their start and end apart: 6, of which 4 were waited for; matrix products, arithmetic and copies ran while one was open for 1% of the time, Pallas kernels for 5%

profile of v4, /device:TPU:1, one launch (start us, length us, event | category | flops | bytes accessed | tf_op | source)
XLA Modules:
  0.0 182.7 jit_solution(9725640653883191688)
XLA Ops:
  7.2 0.0 all-gather.2.cloned.1.call-start
  7.2 2.8 %sort_units.1 = (bf16[16,2,32,128]{3,2,1,0:T(8,128)(2,1)S(1)}, bf16[16,2,32,128]{3,2,1,0:T(8,128)(2,1)S(1)}, s32[1,1024]{1,0:T(1,128)S(1)}) custom-call(s32[1]{0:T(128)} %bitcast.1.core_ref, s32[1,1024]{1,0:T(1,128)} %bitcast.17, bf16[128,1024]{1,0:T(8,128)(2,1)} %w_in_hbm.1, bf16[1024,128]{1,0:T(8,128)(2,1)} %w_out_hbm.1), custom_call_target="tpu_custom_call" | custom-call | tf_op jit(solution)/shard_map/sort_units/pallas_call | solution.py:264
  10.1 3.3 %collective-permute-start.1 = (bf16[16,2,32,128]{3,2,1,0:T(8,128)(2,1)S(1)}, bf16[16,2,32,128]{3,2,1,0:T(8,128)(2,1)S(1)}, u32[]{:S(2)}, u32[]{:S(2)}) collective-permute-start(bf16[16,2,32,128]{3,2,1,0:T(8,128)(2,1)S(1)} %get-tuple-element.16), channel_id=1, source_target_pairs={{0,16},{16,0},{1,17},{17,1},{2,18},{18,2},{3,19},{19,3},{4,20},{20... | collective-permute-start | bytes 786440 | tf_op jit(solution)/shard_map/ppermute | solution.py:236
  13.4 1.2 collective-permute-done.1
  14.6 0.3 maximum_select_fusion
  14.8 15.6 %all_to_all.20 = bf16[16,2,32,256]{3,2,1,0:T(8,128)(2,1)} all-to-all(bf16[16,2,32,256]{3,2,1,0:T(8,128)(2,1)S(1)} %maximum_select_fusion), channel_id=1, replica_groups=mesh['z'=8,'core'=2,'y'=4,'x'=4] {'y','x'}, dimensions={0} | all-to-all | bytes 1048576 | tf_op jit(solution)/shard_map/all_to_all | solution.py:240
  30.5 0.0 reduce-scatter.2.cloned.1.call-start
  30.6 0.5 combine_cotangents.1
  31.1 41.8 %all_to_all.21 = bf16[16,2,384,128]{3,2,1,0:T(8,128)(2,1)S(1)} all-to-all(bf16[16,2,384,128]{3,2,1,0:T(8,128)(2,1)S(1)} %combine_cotangents.1), channel_id=1, replica_groups=mesh['z'=8,'core'=2,'y'=4,'x'=4] {'y','x'}, dimensions={0} | all-to-all | bytes 6291456 | tf_op jit(solution)/shard_map/all_to_all | solution.py:240
  72.8 0.4 copy_bitcast_fusion.own_ref
  73.3 2.5 %collective-permute-start = (bf16[2,384,2048]{2,1,0:T(8,128)(2,1)S(1)}, bf16[2,384,2048]{2,1,0:T(8,128)(2,1)}, u32[]{:S(2)}, u32[]{:S(2)}) collective-permute-start(bf16[2,384,2048]{2,1,0:T(8,128)(2,1)S(1)} %copy_bitcast_fusion.own_ref), channel_id=1, source_target_pairs={{0,16},{16,0},{1,17},{17,1},{2,18},{18,2},{3,19},{19,3},{4,20},{20... | collective-permute-start | bytes 9437192 | tf_op jit(solution)/shard_map/ppermute | solution.py:236
  75.8 5.4 %collective-permute-done.peer_ref = bf16[2,384,2048]{2,1,0:T(8,128)(2,1)} collective-permute-done((bf16[2,384,2048]{2,1,0:T(8,128)(2,1)S(1)}, bf16[2,384,2048]{2,1,0:T(8,128)(2,1)}, u32[]{:S(2)}, u32[]{:S(2)}) %collective-permute-start) | collective-permute-done | bytes 3145760 | tf_op jit(solution)/shard_map/ppermute | solution.py:236
  81.2 4.4 %all-gather.2.cloned.1.call-done = bf16[8192,256]{1,0:T(8,128)(2,1)} async-done(((bf16[1024,256]{1,0:T(8,128)(2,1)}), bf16[8192,256]{1,0:T(8,128)(2,1)}) %all-gather.2.cloned.1.call-update) | async-done | bytes 4194320 | tf_op jit(solution)/shard_map/all_gather | solution.py:285
  85.7 13.0 %hidden_and_weight_grads.1 = (bf16[8,16,2,32,256]{4,3,2,1,0:T(8,128)(2,1)}, bf16[16,2,384,128]{3,2,1,0:T(8,128)(2,1)}, bf16[384,512]{1,0:T(8,128)(2,1)}, bf16[384,512]{1,0:T(8,128)(2,1)}) custom-call(bf16[2,384,2048]{2,1,0:T(8,128)(2,1)} %copy-done.5, bf16[2,384,2048]{2,1,0:T(8,128)(2,1)} %collective-permute-done.peer_ref, bf16[8,16,2,32,256]{4,3,2,1,0:T(8,128)(2,1)} %bitcast.12), custom_call_target="tpu_custom_call" | custom-call | flops 8053063680 | bytes 20971520 | tf_op jit(solution)/shard_map/hidden_and_weight_grads/pallas_call | solution.py:300
  98.8 1.0 collective-permute-start.2
  99.7 0.1 copy-done.2
  99.8 6.0 %own_outputs_and_feature_grads.1 = bf16[16,2,384,128]{3,2,1,0:T(8,128)(2,1)S(1)} custom-call(bf16[384,512]{1,0:T(8,128)(2,1)S(1)} %copy-done.1, bf16[384,512]{1,0:T(8,128)(2,1)S(1)} %copy-done.2, bf16[8,16,2,32,256]{4,3,2,1,0:T(8,128)(2,1)} %bitcast.13), custom_call_target="tpu_custom_call" | custom-call | flops 1610612736 | bytes 8388608 | tf_op jit(solution)/shard_map/own_outputs_and_feature_grads/pallas_call | solution.py:334
  105.9 1.1 add_convert_fusion
  107.0 45.0 %all_to_all.22.got_ref.refs_1_ = bf16[16,2,384,128]{3,2,1,0:T(8,128)(2,1)} all-to-all(bf16[16,2,384,128]{3,2,1,0:T(8,128)(2,1)S(1)} %add_convert_fusion), channel_id=1, replica_groups=mesh['z'=8,'core'=2,'y'=4,'x'=4] {'y','x'}, dimensions={0} | all-to-all | bytes 6291456 | tf_op jit(solution)/shard_map/all_to_all | solution.py:240
  152.1 0.8 reduce-scatter.2.cloned.1.call-done
  152.9 17.2 %all_to_all.23 = bf16[16,2,32,256]{3,2,1,0:T(8,128)(2,1)S(1)} all-to-all(bf16[16,2,32,256]{3,2,1,0:T(8,128)(2,1)} %gate.1), channel_id=1, replica_groups=mesh['z'=8,'core'=2,'y'=4,'x'=4] {'y','x'}, dimensions={0} | all-to-all | bytes 1048576 | tf_op jit(solution)/shard_map/all_to_all | solution.py:240
  170.2 2.1 %collective-permute-start.3 = (bf16[16,2,32,128]{3,2,1,0:T(8,128)(2,1)S(1)}, bf16[16,2,32,128]{3,2,1,0:T(8,128)(2,1)S(1)}, u32[]{:S(2)}, u32[]{:S(2)}) collective-permute-start(bf16[16,2,32,128]{3,2,1,0:T(8,128)(2,1)S(1)} %get-tuple-element.26), channel_id=1, source_target_pairs={{0,16},{16,0},{1,17},{17,1},{2,18},{18,2},{3,19},{19,3},{4,20},{20... | collective-permute-start | bytes 786440 | tf_op jit(solution)/shard_map/ppermute | solution.py:236
  172.3 1.8 sum_outputs.1
  174.1 1.8 %unsort_grads.1 = (bf16[128,1024]{1,0:T(8,128)(2,1)}, bf16[1024,128]{1,0:T(8,128)(2,1)}) custom-call(s32[1,1024]{1,0:T(1,128)S(1)} %get-tuple-element.22.places_ref, bf16[16,2,32,128]{3,2,1,0:T(8,128)(2,1)S(1)} %get-tuple-element.27.own_ref, bf16[16,2,32,128]{3,2,1,0:T(8,128)(2,1)S(1)} %collective-permute-done.3.other_ref), custom_call_target="tpu_custom_call" | custom-call | tf_op jit(solution)/shard_map/unsort_grads/pallas_call | solution.py:373
  (17 shorter events, 0.1 us)
Async XLA Ops:
  7.2 23.4 %copy-start.3 = (bf16[4,384,128]{2,1,0:T(8,128)(2,1)S(1)}, bf16[4,384,128]{2,1,0:T(8,128)(2,1)}, u32[]{:S(2)}) copy-start(bf16[4,384,128]{2,1,0:T(8,128)(2,1)} %cot_ref.1) | copy-start | bytes 1179652
  7.2 23.4 %copy-start.4 = (bf16[384,128]{1,0:T(8,128)(2,1)S(1)}, bf16[384,128]{1,0:T(8,128)(2,1)}, u32[]{:S(2)}) copy-start(bf16[384,128]{1,0:T(8,128)(2,1)} %x_ref.1) | copy-start | bytes 294916
  7.2 78.5 %all-gather.2.cloned.1.call-start = ((), (), s32[]{:S(2)}) async-start(), calls=%async_computation.5 | async-start | bytes 4718592 | tf_op jit(solution)/shard_map/all_gather | solution.py:285
  10.1 4.5 %collective-permute-start.1 = (bf16[16,2,32,128]{3,2,1,0:T(8,128)(2,1)S(1)}, bf16[16,2,32,128]{3,2,1,0:T(8,128)(2,1)S(1)}, u32[]{:S(2)}, u32[]{:S(2)}) collective-permute-start(bf16[16,2,32,128]{3,2,1,0:T(8,128)(2,1)S(1)} %get-tuple-element.16), channel_id=1, source_target_pairs={{0,16},{16,0},{1,17},{17,1},{2,18},{18,2},{3,19},{19,3},{4,20},{20... | collective-permute-start | bytes 786440 | tf_op jit(solution)/shard_map/ppermute | solution.py:236
  30.5 122.4 %reduce-scatter.2.cloned.1.call-start = ((), (), s32[]{:S(2)}) async-start(), calls=%async_computation.6 | async-start | bytes 4718592 | tf_op jit(solution)/shard_map/reduce_scatter | solution.py:331
  73.3 12.4 %copy-start.5 = (bf16[2,384,2048]{2,1,0:T(8,128)(2,1)}, bf16[2,384,2048]{2,1,0:T(8,128)(2,1)S(1)}, u32[]{:S(2)}) copy-start(bf16[2,384,2048]{2,1,0:T(8,128)(2,1)S(1)} %copy_bitcast_fusion.own_ref) | copy-start | bytes 9437188
  73.3 8.0 %collective-permute-start = (bf16[2,384,2048]{2,1,0:T(8,128)(2,1)S(1)}, bf16[2,384,2048]{2,1,0:T(8,128)(2,1)}, u32[]{:S(2)}, u32[]{:S(2)}) collective-permute-start(bf16[2,384,2048]{2,1,0:T(8,128)(2,1)S(1)} %copy_bitcast_fusion.own_ref), channel_id=1, source_target_pairs={{0,16},{16,0},{1,17},{17,1},{2,18},{18,2},{3,19},{19,3},{4,20},{20... | collective-permute-start | bytes 9437192 | tf_op jit(solution)/shard_map/ppermute | solution.py:236
  98.7 1.0 copy-start.1
  98.7 1.1 copy-start.2
  98.8 7.1 %collective-permute-start.2 = (bf16[16,2,384,128]{3,2,1,0:T(8,128)(2,1)}, bf16[16,2,384,128]{3,2,1,0:T(8,128)(2,1)S(1)}, u32[]{:S(2)}, u32[]{:S(2)}) collective-permute-start(bf16[16,2,384,128]{3,2,1,0:T(8,128)(2,1)} %get-tuple-element.19), channel_id=1, source_target_pairs={{0,16},{16,0},{1,17},{17,1},{2,18},{18,2},{3,19},{19,3},{4,20},{20... | collective-permute-start | bytes 9437192 | tf_op jit(solution)/shard_map/ppermute | solution.py:236
  152.9 19.4 %copy-start = (bf16[16,2,384,128]{3,2,1,0:T(8,128)(2,1)S(1)}, bf16[16,2,384,128]{3,2,1,0:T(8,128)(2,1)}, u32[]{:S(2)}) copy-start(bf16[16,2,384,128]{3,2,1,0:T(8,128)(2,1)} %all_to_all.22.got_ref.refs_1_) | copy-start | bytes 9437188
  170.2 3.9 %collective-permute-start.3 = (bf16[16,2,32,128]{3,2,1,0:T(8,128)(2,1)S(1)}, bf16[16,2,32,128]{3,2,1,0:T(8,128)(2,1)S(1)}, u32[]{:S(2)}, u32[]{:S(2)}) collective-permute-start(bf16[16,2,32,128]{3,2,1,0:T(8,128)(2,1)S(1)} %get-tuple-element.26), channel_id=1, source_target_pairs={{0,16},{16,0},{1,17},{17,1},{2,18},{18,2},{3,19},{19,3},{4,20},{20... | collective-permute-start | bytes 786440 | tf_op jit(solution)/shard_map/ppermute | solution.py:236
Sparse Core Ops, SparseCore 0:
  30.6 54.9 all-gather.1
  98.9 53.9 reduce-scatter.1

commit v5 on v4

--- a/solution.py
+++ b/solution.py
@@ -29,8 +29,9 @@
 
 
 def one_hot(places):
-    size = places.shape[1]
-    return (lax.broadcasted_iota(jnp.int32, (size, size), 0) == places).astype(BF16)
+    rows, lanes = places.shape
+    number = lax.broadcasted_iota(jnp.int32, (rows * lanes, lanes), 0)
+    return jnp.concatenate([(number == places[r : r + 1]).astype(BF16) for r in range(rows)], axis=1)
 
 
 def sort_kernel(
@@ -46,21 +47,28 @@
         load.start()
     first.wait()
     units = units_ref[...]
-    size = units.shape[1]
     band = (
         (units >= FF // 8).astype(jnp.int32)
         + (units >= FF // 4).astype(jnp.int32)
         + (units >= FF // 2).astype(jnp.int32)
     )
-    rows = lax.broadcasted_iota(jnp.int32, (8, size), 0)
-    member = rows == band
+    count, lanes = band.shape
+    members = [band == b for b in range(4)]
+    stacked = jnp.concatenate([member.astype(F32) for member in members], axis=0)
     before = (
-        lax.broadcasted_iota(jnp.int32, (size, size), 0)
-        < lax.broadcasted_iota(jnp.int32, (size, size), 1)
+        lax.broadcasted_iota(jnp.int32, (lanes, lanes), 0) < lax.broadcasted_iota(jnp.int32, (lanes, lanes), 1)
     ).astype(BF16)
-    count = jnp.dot(member.astype(BF16), before, preferred_element_type=F32)
-    base = jnp.where(rows == 0, 0, jnp.where(rows == 1, size // 8, jnp.where(rows == 2, size // 4, size // 2)))
-    rank = jnp.sum(jnp.where(member, count + base.astype(F32), 0.0), axis=0, keepdims=True).astype(jnp.int32)
+    within_row = jnp.dot(stacked.astype(BF16), before, preferred_element_type=F32)
+    totals = jnp.sum(stacked, axis=1, keepdims=True)
+    size = count * lanes
+    ranks = [jnp.zeros((1, lanes), F32)] * count
+    for b, base in enumerate((0, size // 8, size // 4, size // 2)):
+        so_far = jnp.full((1, 1), base, F32)
+        for r in range(count):
+            row = slice(b * count + r, b * count + r + 1)
+            ranks[r] = ranks[r] + stacked[row] * (within_row[row] + so_far)
+            so_far = so_far + totals[row]
+    rank = jnp.concatenate(ranks, axis=0).astype(jnp.int32)
     dest = rank // SHARE
     within = rank % SHARE
     half = within // HALF
@@ -232,6 +240,10 @@
     return pltpu.with_memory_space_constraint(value, pltpu.HBM)
 
 
+def in_vmem(value):
+    return pltpu.with_memory_space_constraint(value, pltpu.VMEM)
+
+
 def to_other_core(value):
     return lax.ppermute(value, "core", [(0, 1), (1, 0)])
 
@@ -266,19 +278,19 @@
         out_shape=(
             struct(MP, 2, HALF, part),
             struct(MP, 2, HALF, part),
-            struct(1, units, dtype=jnp.int32),
+            struct(units // part, part, dtype=jnp.int32),
         ),
         in_specs=[SMEM, ANY, ANY, ANY],
         out_specs=(VMEM, VMEM, VMEM),
         scratch_shapes=[
-            pltpu.VMEM((1, units), jnp.int32),
+            pltpu.VMEM((units // part, part), jnp.int32),
             pltpu.VMEM(w_in.shape, BF16),
             pltpu.VMEM(w_out.shape, BF16),
             pltpu.SemaphoreType.DMA((3,)),
         ],
         compiler_params=params(),
         name="sort_units",
-    )(core.reshape(1), *map(in_hbm, (unit_order.reshape(1, units), w_in, w_out)))
+    )(core.reshape(1), *map(in_hbm, (unit_order.reshape(-1, part), w_in, w_out)))
     got = to_other_core(other)
     both = jnp.where(core == 0, jnp.concatenate([own, got], axis=3), jnp.concatenate([got, own], axis=3))
     mine = exchange(both)
@@ -302,8 +314,8 @@
         out_shape=(
             struct(Z, MP, 2, HALF, width),
             struct(MP, 2, count, part),
-            struct(count, UNITS),
-            struct(count, UNITS),
+            pltpu.VMEM((count, UNITS), BF16),
+            pltpu.VMEM((count, UNITS), BF16),
         ),
         in_specs=[ANY] * 3,
         out_specs=(ANY,) * 4,
@@ -348,7 +360,7 @@
         compiler_params=params(50),
         cost_estimate=pl.CostEstimate(flops=4 * UNITS * count * full, bytes_accessed=8 << 20, transcendentals=0),
         name="own_outputs_and_feature_grads",
-    )(hidden, grad_pre, weights)
+    )(in_vmem(hidden), in_vmem(grad_pre), weights)
     out_peer = to_other_core(out_other)
     out_sum = (out_own.astype(F32) + out_peer.astype(F32)).astype(BF16)
     out_got = exchange(out_sum)

time: 183 us -> 183 us (level)
  waiting for transfers between devices: 11.9 us -> 9.94 us
where the time goes in v5:
time: 183 us
  blocking collectives  120 us (66%)
  Pallas kernels  26.4 us (14%)
  between operations  14.2 us (8%)
  waiting for transfers between devices  9.94 us (5%)
  starting transfers between devices  8.55 us (5%)
  local copies, waits for them, and re-layouts  2.19 us (1%)
    all_to_all x4, blocking collectives, exchange(): return lax.all_to_all(value, ('y', 'x'), 0, 0, tiled=True)  120 us
    pallas_call x1, Pallas kernels, per_device(): pl.pallas_call(grads_kernel, out_shape=(struct(Z, MP, 2, HALF, width), st...  13.5 us
    ppermute x4, starting transfers between devices, to_other_core(): return lax.ppermute(value, 'core', [(0, 1), (1, 0)])  8.47 us
    ppermute x4, waiting for transfers between devices, to_other_core(): return lax.ppermute(value, 'core', [(0, 1), (1, 0)])  6.59 us
    pallas_call x1, Pallas kernels, per_device(): pl.pallas_call(own_kernel, out_shape=struct(MP, 2, count, part), in_specs...  6.04 us
  transfers between devices with their start and end apart: 6, of which 4 were waited for; matrix products, arithmetic and copies ran while one was open for 1% of the time, Pallas kernels for 5%

profile of v5, /device:TPU:1, one launch (start us, length us, event | category | flops | bytes accessed | tf_op | source)
XLA Modules:
  0.0 183.1 jit_solution(15780146314772868039)
XLA Ops:
  7.2 0.0 all-gather.2.cloned.1.call-start
  7.2 2.8 %sort_units.1 = (bf16[16,2,32,128]{3,2,1,0:T(8,128)(2,1)S(1)}, bf16[16,2,32,128]{3,2,1,0:T(8,128)(2,1)S(1)}, s32[8,128]{1,0:T(8,128)S(1)}) custom-call(s32[1]{0:T(128)} %bitcast.1.core_ref, s32[8,128]{1,0:T(8,128)} %bitcast.17, bf16[128,1024]{1,0:T(8,128)(2,1)} %w_in_hbm.1, bf16[1024,128]{1,0:T(8,128)(2,1)} %w_out_hbm.1), custom_call_target="tpu_custom_call" | custom-call | tf_op jit(solution)/shard_map/sort_units/pallas_call | solution.py:276
  10.0 3.3 %collective-permute-start.1 = (bf16[16,2,32,128]{3,2,1,0:T(8,128)(2,1)S(1)}, bf16[16,2,32,128]{3,2,1,0:T(8,128)(2,1)S(1)}, u32[]{:S(2)}, u32[]{:S(2)}) collective-permute-start(bf16[16,2,32,128]{3,2,1,0:T(8,128)(2,1)S(1)} %get-tuple-element.16), channel_id=1, source_target_pairs={{0,16},{16,0},{1,17},{17,1},{2,18},{18,2},{3,19},{19,3},{4,20},{20... | collective-permute-start | bytes 786440 | tf_op jit(solution)/shard_map/ppermute | solution.py:248
  13.3 1.2 collective-permute-done.1
  14.5 0.3 maximum_select_fusion
  14.8 15.6 %all_to_all.20 = bf16[16,2,32,256]{3,2,1,0:T(8,128)(2,1)} all-to-all(bf16[16,2,32,256]{3,2,1,0:T(8,128)(2,1)S(1)} %maximum_select_fusion), channel_id=1, replica_groups=mesh['z'=8,'core'=2,'y'=4,'x'=4] {'y','x'}, dimensions={0} | all-to-all | bytes 1048576 | tf_op jit(solution)/shard_map/all_to_all | solution.py:252
  30.4 0.0 reduce-scatter.2.cloned.1.call-start
  30.5 0.5 combine_cotangents.1
  31.0 41.8 %all_to_all.21 = bf16[16,2,384,128]{3,2,1,0:T(8,128)(2,1)S(1)} all-to-all(bf16[16,2,384,128]{3,2,1,0:T(8,128)(2,1)S(1)} %combine_cotangents.1), channel_id=1, replica_groups=mesh['z'=8,'core'=2,'y'=4,'x'=4] {'y','x'}, dimensions={0} | all-to-all | bytes 6291456 | tf_op jit(solution)/shard_map/all_to_all | solution.py:252
  72.7 0.4 copy_bitcast_fusion.own_ref
  73.2 1.7 copy-done.3
  74.9 2.3 %collective-permute-start = (bf16[2,384,2048]{2,1,0:T(8,128)(2,1)S(1)}, bf16[2,384,2048]{2,1,0:T(8,128)(2,1)}, u32[]{:S(2)}, u32[]{:S(2)}) collective-permute-start(bf16[2,384,2048]{2,1,0:T(8,128)(2,1)S(1)} %copy_bitcast_fusion.own_ref), channel_id=1, source_target_pairs={{0,16},{16,0},{1,17},{17,1},{2,18},{18,2},{3,19},{19,3},{4,20},{20... | collective-permute-start | bytes 9437192 | tf_op jit(solution)/shard_map/ppermute | solution.py:248
  77.2 5.4 %collective-permute-done.peer_ref = bf16[2,384,2048]{2,1,0:T(8,128)(2,1)} collective-permute-done((bf16[2,384,2048]{2,1,0:T(8,128)(2,1)S(1)}, bf16[2,384,2048]{2,1,0:T(8,128)(2,1)}, u32[]{:S(2)}, u32[]{:S(2)}) %collective-permute-start) | collective-permute-done | bytes 3145760 | tf_op jit(solution)/shard_map/ppermute | solution.py:248
  82.6 3.0 %all-gather.2.cloned.1.call-done = bf16[8192,256]{1,0:T(8,128)(2,1)} async-done(((bf16[1024,256]{1,0:T(8,128)(2,1)}), bf16[8192,256]{1,0:T(8,128)(2,1)}) %all-gather.2.cloned.1.call-update) | async-done | bytes 4194320 | tf_op jit(solution)/shard_map/all_gather | solution.py:297
  85.6 13.5 %hidden_and_weight_grads.1 = (bf16[8,16,2,32,256]{4,3,2,1,0:T(8,128)(2,1)}, bf16[16,2,384,128]{3,2,1,0:T(8,128)(2,1)}, bf16[384,512]{1,0:T(8,128)(2,1)S(1)}, bf16[384,512]{1,0:T(8,128)(2,1)S(1)}) custom-call(bf16[2,384,2048]{2,1,0:T(8,128)(2,1)} %copy-done.3, bf16[2,384,2048]{2,1,0:T(8,128)(2,1)} %collective-permute-done.peer_ref, ...), custom_call_target="tpu_custom_call" | custom-call | flops 8053063680 | bytes 20971520 | tf_op jit(solution)/shard_map/hidden_and_weight_grads/pallas_call | solution.py:312
  99.1 0.8 collective-permute-start.2
  99.9 6.0 %own_outputs_and_feature_grads.1 = bf16[16,2,384,128]{3,2,1,0:T(8,128)(2,1)S(1)} custom-call(bf16[384,512]{1,0:T(8,128)(2,1)S(1)} %get-tuple-element.17.hidden_ref, bf16[384,512]{1,0:T(8,128)(2,1)S(1)} %get-tuple-element.18.grad_pre_ref, bf16[8,16,2,32,256]{4,3,2,1,0:T(8,128)(2,1)} %bitcast.13), custom_call_target="tpu_custom_call" | custom-call | flops 1610612736 | bytes 8388608 | tf_op jit(solution)/shard_map/own_outputs_and_feature_grads/pallas_call | solution.py:346
  105.9 1.1 add_convert_fusion
  107.1 45.8 %all_to_all.22.got_ref.refs_1_ = bf16[16,2,384,128]{3,2,1,0:T(8,128)(2,1)} all-to-all(bf16[16,2,384,128]{3,2,1,0:T(8,128)(2,1)S(1)} %add_convert_fusion), channel_id=1, replica_groups=mesh['z'=8,'core'=2,'y'=4,'x'=4] {'y','x'}, dimensions={0} | all-to-all | bytes 6291456 | tf_op jit(solution)/shard_map/all_to_all | solution.py:252
  152.9 0.4 reduce-scatter.2.cloned.1.call-done
  153.2 17.3 %all_to_all.23 = bf16[16,2,32,256]{3,2,1,0:T(8,128)(2,1)S(1)} all-to-all(bf16[16,2,32,256]{3,2,1,0:T(8,128)(2,1)} %gate.1), channel_id=1, replica_groups=mesh['z'=8,'core'=2,'y'=4,'x'=4] {'y','x'}, dimensions={0} | all-to-all | bytes 1048576 | tf_op jit(solution)/shard_map/all_to_all | solution.py:252
  170.5 2.1 %collective-permute-start.3 = (bf16[16,2,32,128]{3,2,1,0:T(8,128)(2,1)S(1)}, bf16[16,2,32,128]{3,2,1,0:T(8,128)(2,1)S(1)}, u32[]{:S(2)}, u32[]{:S(2)}) collective-permute-start(bf16[16,2,32,128]{3,2,1,0:T(8,128)(2,1)S(1)} %get-tuple-element.26), channel_id=1, source_target_pairs={{0,16},{16,0},{1,17},{17,1},{2,18},{18,2},{3,19},{19,3},{4,20},{20... | collective-permute-start | bytes 786440 | tf_op jit(solution)/shard_map/ppermute | solution.py:248
  172.7 1.8 sum_outputs.1
  174.4 1.8 %unsort_grads.1 = (bf16[128,1024]{1,0:T(8,128)(2,1)}, bf16[1024,128]{1,0:T(8,128)(2,1)}) custom-call(s32[8,128]{1,0:T(8,128)S(1)} %get-tuple-element.22.places_ref, bf16[16,2,32,128]{3,2,1,0:T(8,128)(2,1)S(1)} %get-tuple-element.27.own_ref, bf16[16,2,32,128]{3,2,1,0:T(8,128)(2,1)S(1)} %collective-permute-done.3.other_ref), custom_call_target="tpu_custom_call" | custom-call | tf_op jit(solution)/shard_map/unsort_grads/pallas_call | solution.py:385
  (13 shorter events, 0.1 us)
Async XLA Ops:
  7.2 23.3 %copy-start.1 = (bf16[4,384,128]{2,1,0:T(8,128)(2,1)S(1)}, bf16[4,384,128]{2,1,0:T(8,128)(2,1)}, u32[]{:S(2)}) copy-start(bf16[4,384,128]{2,1,0:T(8,128)(2,1)} %cot_ref.1) | copy-start | bytes 1179652
  7.2 23.3 %copy-start.2 = (bf16[384,128]{1,0:T(8,128)(2,1)S(1)}, bf16[384,128]{1,0:T(8,128)(2,1)}, u32[]{:S(2)}) copy-start(bf16[384,128]{1,0:T(8,128)(2,1)} %x_ref.1) | copy-start | bytes 294916
  7.2 78.4 %all-gather.2.cloned.1.call-start = ((), (), s32[]{:S(2)}) async-start(), calls=%async_computation.5 | async-start | bytes 4718592 | tf_op jit(solution)/shard_map/all_gather | solution.py:297
  10.0 4.5 %collective-permute-start.1 = (bf16[16,2,32,128]{3,2,1,0:T(8,128)(2,1)S(1)}, bf16[16,2,32,128]{3,2,1,0:T(8,128)(2,1)S(1)}, u32[]{:S(2)}, u32[]{:S(2)}) collective-permute-start(bf16[16,2,32,128]{3,2,1,0:T(8,128)(2,1)S(1)} %get-tuple-element.16), channel_id=1, source_target_pairs={{0,16},{16,0},{1,17},{17,1},{2,18},{18,2},{3,19},{19,3},{4,20},{20... | collective-permute-start | bytes 786440 | tf_op jit(solution)/shard_map/ppermute | solution.py:248
  30.4 122.8 %reduce-scatter.2.cloned.1.call-start = ((), (), s32[]{:S(2)}) async-start(), calls=%async_computation.6 | async-start | bytes 4718592 | tf_op jit(solution)/shard_map/reduce_scatter | solution.py:343
  73.2 1.7 copy-start.3
  74.9 7.7 %collective-permute-start = (bf16[2,384,2048]{2,1,0:T(8,128)(2,1)S(1)}, bf16[2,384,2048]{2,1,0:T(8,128)(2,1)}, u32[]{:S(2)}, u32[]{:S(2)}) collective-permute-start(bf16[2,384,2048]{2,1,0:T(8,128)(2,1)S(1)} %copy_bitcast_fusion.own_ref), channel_id=1, source_target_pairs={{0,16},{16,0},{1,17},{17,1},{2,18},{18,2},{3,19},{19,3},{4,20},{20... | collective-permute-start | bytes 9437192 | tf_op jit(solution)/shard_map/ppermute | solution.py:248
  99.1 6.8 %collective-permute-start.2 = (bf16[16,2,384,128]{3,2,1,0:T(8,128)(2,1)}, bf16[16,2,384,128]{3,2,1,0:T(8,128)(2,1)S(1)}, u32[]{:S(2)}, u32[]{:S(2)}) collective-permute-start(bf16[16,2,384,128]{3,2,1,0:T(8,128)(2,1)} %get-tuple-element.19), channel_id=1, source_target_pairs={{0,16},{16,0},{1,17},{17,1},{2,18},{18,2},{3,19},{19,3},{4,20},{20... | collective-permute-start | bytes 9437192 | tf_op jit(solution)/shard_map/ppermute | solution.py:248
  153.2 19.4 %copy-start = (bf16[16,2,384,128]{3,2,1,0:T(8,128)(2,1)S(1)}, bf16[16,2,384,128]{3,2,1,0:T(8,128)(2,1)}, u32[]{:S(2)}) copy-start(bf16[16,2,384,128]{3,2,1,0:T(8,128)(2,1)} %all_to_all.22.got_ref.refs_1_) | copy-start | bytes 9437188
  170.5 3.9 %collective-permute-start.3 = (bf16[16,2,32,128]{3,2,1,0:T(8,128)(2,1)S(1)}, bf16[16,2,32,128]{3,2,1,0:T(8,128)(2,1)S(1)}, u32[]{:S(2)}, u32[]{:S(2)}) collective-permute-start(bf16[16,2,32,128]{3,2,1,0:T(8,128)(2,1)S(1)} %get-tuple-element.26), channel_id=1, source_target_pairs={{0,16},{16,0},{1,17},{17,1},{2,18},{18,2},{3,19},{19,3},{4,20},{20... | collective-permute-start | bytes 786440 | tf_op jit(solution)/shard_map/ppermute | solution.py:248
Sparse Core Ops, SparseCore 0:
  30.5 54.9 all-gather.1
  99.2 53.9 reduce-scatter.1

commit v6 on v5

--- a/solution.py
+++ b/solution.py
@@ -364,16 +364,11 @@
     out_peer = to_other_core(out_other)
     out_sum = (out_own.astype(F32) + out_peer.astype(F32)).astype(BF16)
     out_got = exchange(out_sum)
-    rows = 128
     outputs, grad_features = pl.pallas_call(
         sums_kernel,
-        grid=(count // rows,),
         out_shape=(struct(4, count, part), struct(count, part)),
-        in_specs=[pl.BlockSpec((MP, 2, rows, part), lambda t: (0, 0, t, 0))],
-        out_specs=(
-            pl.BlockSpec((4, rows, part), lambda t: (0, t, 0)),
-            pl.BlockSpec((rows, part), lambda t: (t, 0)),
-        ),
+        in_specs=[VMEM],
+        out_specs=(VMEM, VMEM),
         compiler_params=params(),
         name="sum_outputs",
     )(out_got)

time: 183 us -> 183 us (level)
  transfers between devices with their start and end apart: 6 -> 6, of which waited for: 4 -> 5; matrix products, arithmetic and copies ran while one was open for 1% -> 1% of each run, Pallas kernels for 5% -> 4%
where the time goes in v6:
time: 183 us; the launch traced here: 182 us
  blocking collectives  120 us (66%)
  Pallas kernels  25.7 us (14%)
  between operations  14.2 us (8%)
  waiting for transfers between devices  10 us (5%)
  starting transfers between devices  8.55 us (5%)
  local copies, waits for them, and re-layouts  2.19 us (1%)
    all_to_all x4, blocking collectives, exchange(): return lax.all_to_all(value, ('y', 'x'), 0, 0, tiled=True)  120 us
    pallas_call x1, Pallas kernels, per_device(): pl.pallas_call(grads_kernel, out_shape=(struct(Z, MP, 2, HALF, width), st...  13.5 us
    ppermute x4, starting transfers between devices, to_other_core(): return lax.ppermute(value, 'core', [(0, 1), (1, 0)])  8.47 us
    ppermute x4, waiting for transfers between devices, to_other_core(): return lax.ppermute(value, 'core', [(0, 1), (1, 0)])  6.68 us
    pallas_call x1, Pallas kernels, per_device(): pl.pallas_call(own_kernel, out_shape=struct(MP, 2, count, part), in_specs...  6.04 us
  transfers between devices with their start and end apart: 6, of which 5 were waited for; matrix products, arithmetic and copies ran while one was open for 1% of the time, Pallas kernels for 4%

profile of v6, /device:TPU:1, one launch (start us, length us, event | category | flops | bytes accessed | tf_op | source)
XLA Modules:
  0.0 182.5 jit_solution(6280892378861819914)
XLA Ops:
  7.2 2.8 %sort_units.1 = (bf16[16,2,32,128]{3,2,1,0:T(8,128)(2,1)S(1)}, bf16[16,2,32,128]{3,2,1,0:T(8,128)(2,1)S(1)}, s32[8,128]{1,0:T(8,128)S(1)}) custom-call(s32[1]{0:T(128)} %bitcast.1.core_ref, s32[8,128]{1,0:T(8,128)} %bitcast.17, bf16[128,1024]{1,0:T(8,128)(2,1)} %w_in_hbm.1, bf16[1024,128]{1,0:T(8,128)(2,1)} %w_out_hbm.1), custom_call_target="tpu_custom_call" | custom-call | tf_op jit(solution)/shard_map/sort_units/pallas_call | solution.py:276
  10.0 3.3 %collective-permute-start.1 = (bf16[16,2,32,128]{3,2,1,0:T(8,128)(2,1)S(1)}, bf16[16,2,32,128]{3,2,1,0:T(8,128)(2,1)S(1)}, u32[]{:S(2)}, u32[]{:S(2)}) collective-permute-start(bf16[16,2,32,128]{3,2,1,0:T(8,128)(2,1)S(1)} %get-tuple-element.16), channel_id=1, source_target_pairs={{0,16},{16,0},{1,17},{17,1},{2,18},{18,2},{3,19},{19,3},{4,20},{20... | collective-permute-start | bytes 786440 | tf_op jit(solution)/shard_map/ppermute | solution.py:248
  13.3 1.2 collective-permute-done.1
  14.5 0.3 maximum_select_fusion
  14.8 15.6 %all_to_all.20 = bf16[16,2,32,256]{3,2,1,0:T(8,128)(2,1)} all-to-all(bf16[16,2,32,256]{3,2,1,0:T(8,128)(2,1)S(1)} %maximum_select_fusion), channel_id=1, replica_groups=mesh['z'=8,'core'=2,'y'=4,'x'=4] {'y','x'}, dimensions={0} | all-to-all | bytes 1048576 | tf_op jit(solution)/shard_map/all_to_all | solution.py:252
  30.4 0.0 reduce-scatter.2.cloned.1.call-start
  30.5 0.5 combine_cotangents.1
  31.0 41.8 %all_to_all.21 = bf16[16,2,384,128]{3,2,1,0:T(8,128)(2,1)S(1)} all-to-all(bf16[16,2,384,128]{3,2,1,0:T(8,128)(2,1)S(1)} %combine_cotangents.1), channel_id=1, replica_groups=mesh['z'=8,'core'=2,'y'=4,'x'=4] {'y','x'}, dimensions={0} | all-to-all | bytes 6291456 | tf_op jit(solution)/shard_map/all_to_all | solution.py:252
  72.7 0.4 copy_bitcast_fusion.own_ref
  73.2 1.7 copy-done.3
  74.9 2.3 %collective-permute-start = (bf16[2,384,2048]{2,1,0:T(8,128)(2,1)S(1)}, bf16[2,384,2048]{2,1,0:T(8,128)(2,1)}, u32[]{:S(2)}, u32[]{:S(2)}) collective-permute-start(bf16[2,384,2048]{2,1,0:T(8,128)(2,1)S(1)} %copy_bitcast_fusion.own_ref), channel_id=1, source_target_pairs={{0,16},{16,0},{1,17},{17,1},{2,18},{18,2},{3,19},{19,3},{4,20},{20... | collective-permute-start | bytes 9437192 | tf_op jit(solution)/shard_map/ppermute | solution.py:248
  77.2 5.4 %collective-permute-done.peer_ref = bf16[2,384,2048]{2,1,0:T(8,128)(2,1)} collective-permute-done((bf16[2,384,2048]{2,1,0:T(8,128)(2,1)S(1)}, bf16[2,384,2048]{2,1,0:T(8,128)(2,1)}, u32[]{:S(2)}, u32[]{:S(2)}) %collective-permute-start) | collective-permute-done | bytes 3145760 | tf_op jit(solution)/shard_map/ppermute | solution.py:248
  82.6 3.0 %all-gather.2.cloned.1.call-done = bf16[8192,256]{1,0:T(8,128)(2,1)} async-done(((bf16[1024,256]{1,0:T(8,128)(2,1)}), bf16[8192,256]{1,0:T(8,128)(2,1)}) %all-gather.2.cloned.1.call-update) | async-done | bytes 4194320 | tf_op jit(solution)/shard_map/all_gather | solution.py:297
  85.6 13.5 %hidden_and_weight_grads.1 = (bf16[8,16,2,32,256]{4,3,2,1,0:T(8,128)(2,1)}, bf16[16,2,384,128]{3,2,1,0:T(8,128)(2,1)}, bf16[384,512]{1,0:T(8,128)(2,1)S(1)}, bf16[384,512]{1,0:T(8,128)(2,1)S(1)}) custom-call(bf16[2,384,2048]{2,1,0:T(8,128)(2,1)} %copy-done.3, bf16[2,384,2048]{2,1,0:T(8,128)(2,1)} %collective-permute-done.peer_ref, ...), custom_call_target="tpu_custom_call" | custom-call | flops 8053063680 | bytes 20971520 | tf_op jit(solution)/shard_map/hidden_and_weight_grads/pallas_call | solution.py:312
  99.1 0.8 collective-permute-start.2
  99.9 6.0 %own_outputs_and_feature_grads.1 = bf16[16,2,384,128]{3,2,1,0:T(8,128)(2,1)S(1)} custom-call(bf16[384,512]{1,0:T(8,128)(2,1)S(1)} %get-tuple-element.17.hidden_ref, bf16[384,512]{1,0:T(8,128)(2,1)S(1)} %get-tuple-element.18.grad_pre_ref, bf16[8,16,2,32,256]{4,3,2,1,0:T(8,128)(2,1)} %bitcast.13), custom_call_target="tpu_custom_call" | custom-call | flops 1610612736 | bytes 8388608 | tf_op jit(solution)/shard_map/own_outputs_and_feature_grads/pallas_call | solution.py:346
  105.9 1.1 add_convert_fusion
  107.1 45.8 %all_to_all.22.got_ref.refs_1_ = bf16[16,2,384,128]{3,2,1,0:T(8,128)(2,1)} all-to-all(bf16[16,2,384,128]{3,2,1,0:T(8,128)(2,1)S(1)} %add_convert_fusion), channel_id=1, replica_groups=mesh['z'=8,'core'=2,'y'=4,'x'=4] {'y','x'}, dimensions={0} | all-to-all | bytes 6291456 | tf_op jit(solution)/shard_map/all_to_all | solution.py:252
  152.9 0.4 reduce-scatter.2.cloned.1.call-done
  153.2 17.3 %all_to_all.23 = bf16[16,2,32,256]{3,2,1,0:T(8,128)(2,1)S(1)} all-to-all(bf16[16,2,32,256]{3,2,1,0:T(8,128)(2,1)} %gate.1), channel_id=1, replica_groups=mesh['z'=8,'core'=2,'y'=4,'x'=4] {'y','x'}, dimensions={0} | all-to-all | bytes 1048576 | tf_op jit(solution)/shard_map/all_to_all | solution.py:252
  170.5 2.1 %collective-permute-start.3 = (bf16[16,2,32,128]{3,2,1,0:T(8,128)(2,1)S(1)}, bf16[16,2,32,128]{3,2,1,0:T(8,128)(2,1)S(1)}, u32[]{:S(2)}, u32[]{:S(2)}) collective-permute-start(bf16[16,2,32,128]{3,2,1,0:T(8,128)(2,1)S(1)} %get-tuple-element.26), channel_id=1, source_target_pairs={{0,16},{16,0},{1,17},{17,1},{2,18},{18,2},{3,19},{19,3},{4,20},{20... | collective-permute-start | bytes 786440 | tf_op jit(solution)/shard_map/ppermute | solution.py:248
  172.7 1.1 sum_outputs.1
  173.7 0.1 collective-permute-done.3.other_ref
  173.8 1.8 %unsort_grads.1 = (bf16[128,1024]{1,0:T(8,128)(2,1)}, bf16[1024,128]{1,0:T(8,128)(2,1)}) custom-call(s32[8,128]{1,0:T(8,128)S(1)} %get-tuple-element.22.places_ref, bf16[16,2,32,128]{3,2,1,0:T(8,128)(2,1)S(1)} %get-tuple-element.27.own_ref, bf16[16,2,32,128]{3,2,1,0:T(8,128)(2,1)S(1)} %collective-permute-done.3.other_ref), custom_call_target="tpu_custom_call" | custom-call | tf_op jit(solution)/shard_map/unsort_grads/pallas_call | solution.py:380
  (13 shorter events, 0.1 us)
Async XLA Ops:
  7.2 23.3 %copy-start.1 = (bf16[4,384,128]{2,1,0:T(8,128)(2,1)S(1)}, bf16[4,384,128]{2,1,0:T(8,128)(2,1)}, u32[]{:S(2)}) copy-start(bf16[4,384,128]{2,1,0:T(8,128)(2,1)} %cot_ref.1) | copy-start | bytes 1179652
  7.2 23.3 %copy-start.2 = (bf16[384,128]{1,0:T(8,128)(2,1)S(1)}, bf16[384,128]{1,0:T(8,128)(2,1)}, u32[]{:S(2)}) copy-start(bf16[384,128]{1,0:T(8,128)(2,1)} %x_ref.1) | copy-start | bytes 294916
  7.2 78.4 %all-gather.2.cloned.1.call-start = ((), (), s32[]{:S(2)}) async-start(), calls=%async_computation.5 | async-start | bytes 4718592 | tf_op jit(solution)/shard_map/all_gather | solution.py:297
  10.0 4.5 %collective-permute-start.1 = (bf16[16,2,32,128]{3,2,1,0:T(8,128)(2,1)S(1)}, bf16[16,2,32,128]{3,2,1,0:T(8,128)(2,1)S(1)}, u32[]{:S(2)}, u32[]{:S(2)}) collective-permute-start(bf16[16,2,32,128]{3,2,1,0:T(8,128)(2,1)S(1)} %get-tuple-element.16), channel_id=1, source_target_pairs={{0,16},{16,0},{1,17},{17,1},{2,18},{18,2},{3,19},{19,3},{4,20},{20... | collective-permute-start | bytes 786440 | tf_op jit(solution)/shard_map/ppermute | solution.py:248
  30.4 122.8 %reduce-scatter.2.cloned.1.call-start = ((), (), s32[]{:S(2)}) async-start(), calls=%async_computation.6 | async-start | bytes 4718592 | tf_op jit(solution)/shard_map/reduce_scatter | solution.py:343
  73.2 1.7 copy-start.3
  74.9 7.7 %collective-permute-start = (bf16[2,384,2048]{2,1,0:T(8,128)(2,1)S(1)}, bf16[2,384,2048]{2,1,0:T(8,128)(2,1)}, u32[]{:S(2)}, u32[]{:S(2)}) collective-permute-start(bf16[2,384,2048]{2,1,0:T(8,128)(2,1)S(1)} %copy_bitcast_fusion.own_ref), channel_id=1, source_target_pairs={{0,16},{16,0},{1,17},{17,1},{2,18},{18,2},{3,19},{19,3},{4,20},{20... | collective-permute-start | bytes 9437192 | tf_op jit(solution)/shard_map/ppermute | solution.py:248
  99.1 6.8 %collective-permute-start.2 = (bf16[16,2,384,128]{3,2,1,0:T(8,128)(2,1)}, bf16[16,2,384,128]{3,2,1,0:T(8,128)(2,1)S(1)}, u32[]{:S(2)}, u32[]{:S(2)}) collective-permute-start(bf16[16,2,384,128]{3,2,1,0:T(8,128)(2,1)} %get-tuple-element.19), channel_id=1, source_target_pairs={{0,16},{16,0},{1,17},{17,1},{2,18},{18,2},{3,19},{19,3},{4,20},{20... | collective-permute-start | bytes 9437192 | tf_op jit(solution)/shard_map/ppermute | solution.py:248
  153.2 19.4 %copy-start = (bf16[16,2,384,128]{3,2,1,0:T(8,128)(2,1)S(1)}, bf16[16,2,384,128]{3,2,1,0:T(8,128)(2,1)}, u32[]{:S(2)}) copy-start(bf16[16,2,384,128]{3,2,1,0:T(8,128)(2,1)} %all_to_all.22.got_ref.refs_1_) | copy-start | bytes 9437188
  170.5 3.3 %collective-permute-start.3 = (bf16[16,2,32,128]{3,2,1,0:T(8,128)(2,1)S(1)}, bf16[16,2,32,128]{3,2,1,0:T(8,128)(2,1)S(1)}, u32[]{:S(2)}, u32[]{:S(2)}) collective-permute-start(bf16[16,2,32,128]{3,2,1,0:T(8,128)(2,1)S(1)} %get-tuple-element.26), channel_id=1, source_target_pairs={{0,16},{16,0},{1,17},{17,1},{2,18},{18,2},{3,19},{19,3},{4,20},{20... | collective-permute-start | bytes 786440 | tf_op jit(solution)/shard_map/ppermute | solution.py:248
Sparse Core Ops, SparseCore 0:
  30.5 54.9 all-gather.1
  99.2 53.9 reduce-scatter.1
